TPU v7x, 512 devices: a whole 4x8x8 slice. The times are simulated.
512 devices in a mesh: rows: 32 (over z, x_hi, core), rep: 16 (over x_lo, y).
Axes of the slice: x: 4 (x_hi: 2, x_lo: 2; x = x_hi * 2 + x_lo), y: 8, z: 8, core: 2. Of those that a mesh axis runs over, the one named last changes fastest.
Arguments:
- features: bfloat16 [65536, 256], P(('rows', 'rep')), may hold values from -6 to 6
- adjacency: bfloat16 [32, 32, 16, 128, 128], P('rows', 'rep'), may hold values from -0.09375 to 0.09375
- tile_ids: int32 [32, 32, 16], P('rows', 'rep'), may hold values from 0 to 255, as said below
- tile_counts: int32 [32, 32], P('rows', 'rep'), may hold values from 1 to 16, as said below
- weight: bfloat16 [256, 256], replicated, may hold values from -0.375 to 0.375
- grad_out: bfloat16 [65536, 256], P(('rows', 'rep')), may hold values from -6 to 6
Outputs:
- activated: bfloat16 [65536, 256], P(('rows', 'rep'))
- grad_weight: float32 [256, 256], P(None, 'rep')
- grad_features: float32 [32, 2048, 256], P('rep', 'rows')
Inputs may be any that keep to these rules, and one draw needn't show every extreme that they name: `tile_ids`: within one row block and section the 16 entries are distinct; an entry v names tile row v // 16 and tile column v % 16. Only the first tile_counts[r, s] slots of a row block and section hold tiles of the matrix; later slots are padding.
All inputs are finite; a program needn't handle non-finite values.
Results may differ from a plain program's by a relative error of at most 0.025.
Values may be sent and summed in bfloat16 or wider, within the bound.
A program may use at most 64 MiB of HBM per device.

v0:
```python
import jax
import jax.numpy as jnp
from jax import lax
from jax.sharding import PartitionSpec as P


def spread(shard, axis, root):
    mine = lax.axis_index(axis) == root
    return lax.psum(jnp.where(mine, shard, jnp.zeros_like(shard)), axis)


def place_rows(product, slot_ids, tile_count, target, tiles_per):
    live_mask = (jnp.arange(slot_ids.shape[0], dtype=jnp.int32) < tile_count).astype(jnp.float32)
    masked = product * live_mask[:, None, None]
    placed = (
        jnp.zeros((tiles_per, product.shape[1], product.shape[2]), jnp.float32)
        .at[target]
        .add(masked)
    )
    return placed.reshape(tiles_per * product.shape[1], product.shape[2])


def forward_tiles(tile_block, slot_ids, tile_count, section_rows):
    tile_size = tile_block.shape[-1]
    tiles_per = section_rows.shape[0] // tile_size
    row_tile = slot_ids // tiles_per
    col_tile = slot_ids % tiles_per
    blocked = section_rows.reshape(tiles_per, tile_size, section_rows.shape[1])
    picked = jnp.take(blocked, col_tile, axis=0)
    product = jnp.einsum("tij,tjf->tif", tile_block, picked, preferred_element_type=jnp.float32)
    return place_rows(product, slot_ids, tile_count, row_tile, tiles_per)


def backward_tiles(tile_block, slot_ids, tile_count, block_grad):
    tile_size = tile_block.shape[-1]
    tiles_per = block_grad.shape[0] // tile_size
    row_tile = slot_ids // tiles_per
    col_tile = slot_ids % tiles_per
    blocked = block_grad.reshape(tiles_per, tile_size, block_grad.shape[1])
    picked = jnp.take(blocked, row_tile, axis=0)
    product = jnp.einsum("tji,tjf->tif", tile_block, picked, preferred_element_type=jnp.float32)
    return place_rows(product, slot_ids, tile_count, col_tile, tiles_per)


def shards(features, adjacency, tile_ids, tile_counts, weight, grad_out):
    rep_index = lax.axis_index("rep")
    section_dev = adjacency.shape[1]
    slice_rows = features.shape[0]
    width_in = features.shape[1]
    block_rows = slice_rows * lax.axis_size("rep")
    partial_value = jnp.zeros((block_rows, width_in), jnp.float32)
    row_block = lax.all_gather(features, "rep", axis=0, tiled=True)
    for section_num in range(section_dev):
        section_root = rep_index * section_dev + section_num
        section_rows = spread(row_block, "rows", section_root)
        partial_value = partial_value + forward_tiles(
            adjacency[0, section_num],
            tile_ids[0, section_num],
            tile_counts[0, section_num],
            section_rows,
        )
    aggregated = lax.psum_scatter(
        partial_value.astype(jnp.bfloat16), "rep", scatter_dimension=0, tiled=True
    )
    pre_act = jnp.dot(aggregated, weight, preferred_element_type=jnp.float32)
    gate_value = jax.nn.sigmoid(pre_act)
    activated = (pre_act * gate_value).astype(jnp.bfloat16)
    grad_pre = (
        grad_out.astype(jnp.float32) * gate_value * (1.0 + pre_act * (1.0 - gate_value))
    ).astype(jnp.bfloat16)
    weight_term = lax.dot_general(
        aggregated, grad_pre, (((0,), (0,)), ((), ())), preferred_element_type=jnp.float32
    )
    weight_full = lax.psum(weight_term, ("rows", "rep"))
    share_cols = weight_full.shape[1] // lax.axis_size("rep")
    grad_weight = lax.dynamic_slice_in_dim(weight_full, rep_index * share_cols, share_cols, 1)
    grad_agg = lax.dot_general(
        grad_pre, weight, (((1,), (1,)), ((), ())), preferred_element_type=jnp.float32
    ).astype(jnp.bfloat16)
    grad_rows = lax.all_gather(grad_agg, "rep", axis=0, tiled=True)
    column_terms = jnp.stack(
        [
            backward_tiles(
                adjacency[0, section_num],
                tile_ids[0, section_num],
                tile_counts[0, section_num],
                grad_rows,
            ).astype(jnp.bfloat16)
            for section_num in range(section_dev)
        ],
        axis=0,
    )
    grad_features = lax.psum_scatter(column_terms, "rows", scatter_dimension=1, tiled=True).astype(
        jnp.float32
    )
    return (activated, grad_weight, grad_features)


def solution(mesh):
    return jax.shard_map(
        shards,
        mesh=mesh,
        in_specs=(
            P(("rows", "rep"), None),
            P("rows", "rep", None, None, None),
            P("rows", "rep", None),
            P("rows", "rep"),
            P(),
            P(("rows", "rep"), None),
        ),
        out_specs=(P(("rows", "rep"), None), P(None, "rep"), P("rep", "rows", None)),
        check_vma=False,
    )
```

profile of v0, /device:TPU:6, one launch (start us, length us, event | category | flops | bytes accessed | tf_op | source)
XLA Modules:
  0.0 941.7 jit_solution(5202718354391620672)
XLA Ops:
  7.2 0.0 all-gather.3.cloned.1.call-start
  7.2 0.7 all-gather.3.cloned.1.call-update
  7.9 0.0 all-reduce.6.cloned.1.call-start
  8.0 77.9 %all-gather.3.cloned.1.call-done = bf16[2048,256]{1,0:T(8,128)(2,1)} async-done(((bf16[128,256]{1,0:T(8,128)(2,1)}), bf16[2048,256]{1,0:T(8,128)(2,1)}) %all-gather.3.cloned.1.call-update) | async-done | bytes 1048592 | tf_op jit(solution)/shard_map/all_gather | solution.py:52
  85.9 2.7 broadcast_select_fusion
  88.6 0.0 reduce-scatter.3.cloned.1.call-start
  88.7 0.6 fusion.28
  89.2 0.6 compare_convert_fusion
  89.9 0.7 compare_convert_fusion.1
  90.7 272.1 %all-reduce.6.cloned.1.call-done = (bf16[16,128,256]{2,1,0:T(8,128)(2,1)}, bf16[16,128,256]{2,1,0:T(8,128)(2,1)}) async-done(((bf16[16,128,256]{2,1,0:T(8,128)(2,1)}, bf16[16,128,256]{2,1,0:T(8,128)(2,1)}), (bf16[16,128,256]{2,1,0:T(8,128)(2,1)}, bf16[16,128,256]{2,1,0:T(8,128)(2,1)})) %all-reduce.6.cloned.1.call-update) | async-done | bytes 2097168 | tf_op jit(solution)/shard_map/psum | solution.py:9
  362.8 1.8 gather_fusion.1
  364.6 1.6 multiply_bitcast_fusion.2
  366.2 1.8 copy.16
  368.1 1.8 gather_fusion
  369.9 1.6 multiply_bitcast_fusion.3
  371.5 1.9 copy.14
  373.4 0.2 broadcast.275.clone.1
  373.6 3.5 scatter_fusion.1
  377.1 1.5 broadcast.275.clone
  378.7 5.2 scatter_fusion
  383.9 2.8 add_convert_fusion
  386.8 0.0 all-gather.5.cloned.1.call-start
  386.8 76.7 %reduce-scatter.3.cloned.1.call-done = bf16[128,256]{1,0:T(8,128)(2,1)} async-done(((bf16[2048,256]{1,0:T(8,128)(2,1)}), bf16[128,256]{1,0:T(8,128)(2,1)}) %reduce-scatter.3.cloned.1.call-update) | async-done | bytes 65552 | tf_op jit(solution)/shard_map/reduce_scatter | solution.py:62
  463.5 1.7 multiply_convert_fusion
  465.2 0.8 convolution_convert_fusion
  466.0 0.0 all-reduce.4.cloned.1.call-start
  466.1 1.8 fusion.29
  467.9 0.0 reduce-scatter.5.cloned.1.call-start
  467.9 66.4 %all-gather.5.cloned.1.call-done = bf16[2048,256]{1,0:T(8,128)(2,1)} async-done(((bf16[128,256]{1,0:T(8,128)(2,1)}), bf16[2048,256]{1,0:T(8,128)(2,1)}) %all-gather.5.cloned.1.call-update) | async-done | bytes 1048592 | tf_op jit(solution)/shard_map/all_gather | solution.py:80
  534.3 1.8 gather_fusion.2
  536.2 1.6 multiply_bitcast_fusion.1
  537.8 1.9 copy.18
  539.7 0.2 broadcast.275.clone.3
  539.9 3.5 scatter_fusion.2
  543.4 1.1 convert_element_type.71
  544.5 0.5 copy-done.1
  545.0 1.6 gather_fusion.3
  546.6 1.9 multiply_bitcast_fusion
  548.5 1.9 copy.20
  550.4 0.2 broadcast.275.clone.2
  550.6 3.5 scatter_fusion.3
  554.1 0.1 convert_element_type.73
  554.3 1.1 copy-done.2
  555.3 1.5 pad_maximum_fusion
  556.9 246.2 %all-reduce.4.cloned.1.call-done = f32[256,256]{0,1:T(8,128)} async-done(((f32[256,256]{0,1:T(8,128)}), f32[256,256]{0,1:T(8,128)}) %all-reduce.4.cloned.1.call-update) | async-done | bytes 262160 | tf_op jit(solution)/shard_map/psum | solution.py:74
  803.1 1.3 constant_dynamic-slice_fusion
  804.4 129.0 %reduce-scatter.5.cloned.1.call-done = bf16[2,64,256]{2,1,0:T(8,128)(2,1)} async-done(((bf16[2,2048,256]{2,1,0:T(8,128)(2,1)}), bf16[2,64,256]{2,1,0:T(8,128)(2,1)}) %reduce-scatter.5.cloned.1.call-update) | async-done | bytes 65552 | tf_op jit(solution)/shard_map/reduce_scatter | solution.py:93
  933.4 1.5 convert_element_type.75
  (22 shorter events, 0.2 us)
Async XLA Ops:
  7.2 456.3 %copy-start = (bf16[256,256]{1,0:T(8,128)(2,1)S(1)}, bf16[256,256]{1,0:T(8,128)(2,1)}, u32[]{:S(2)}) copy-start(bf16[256,256]{1,0:T(8,128)(2,1)} %param.12) | copy-start | bytes 393220
  7.2 78.7 %all-gather.3.cloned.1.call-start = ((), (), s32[]{:S(2)}) async-start(), calls=%async_computation.2 | async-start | bytes 1114112 | tf_op jit(solution)/shard_map/all_gather | solution.py:52
  7.9 354.8 %all-reduce.6.cloned.1.call-start = ((), (), s32[]{:S(2)}) async-start(), calls=%async_computation.7 | async-start | bytes 4194304 | tf_op jit(solution)/shard_map/psum | solution.py:9
  8.0 80.7 %copy-start.4 = (s32[1,2]{1,0:T(1,128)S(1)}, s32[1,2]{1,0:T(1,128)}, u32[]{:S(2)}) copy-start(s32[1,2]{1,0:T(1,128)} %param.11) | copy-start | bytes 28
  8.0 82.6 %copy-start.3 = (s32[1,2,16]{2,1,0:T(2,128)S(1)}, s32[1,2,16]{2,1,0:T(2,128)}, u32[]{:S(2)}) copy-start(s32[1,2,16]{2,1,0:T(2,128)} %param.10) | copy-start | bytes 388
  88.6 374.9 %reduce-scatter.3.cloned.1.call-start = ((), (), s32[]{:S(2)}) async-start(), calls=%async_computation.3 | async-start | bytes 1114112 | tf_op jit(solution)/shard_map/reduce_scatter | solution.py:62
  383.9 79.6 %copy-start.5 = (bf16[128,256]{1,0:T(8,128)(2,1)S(1)}, bf16[128,256]{1,0:T(8,128)(2,1)}, u32[]{:S(2)}) copy-start(bf16[128,256]{1,0:T(8,128)(2,1)} %param.13) | copy-start | bytes 196612
  386.8 147.6 %all-gather.5.cloned.1.call-start = ((), (), s32[]{:S(2)}) async-start(), calls=%async_computation.5 | async-start | bytes 1114112 | tf_op jit(solution)/shard_map/all_gather | solution.py:80
  466.0 337.0 %all-reduce.4.cloned.1.call-start = ((), (), s32[]{:S(2)}) async-start(), calls=%async_computation.4 | async-start | bytes 524288 | tf_op jit(solution)/shard_map/psum | solution.py:74
  467.9 465.5 %reduce-scatter.5.cloned.1.call-start = ((), (), s32[]{:S(2)}) async-start(), calls=%async_computation.6 | async-start | bytes 2162688 | tf_op jit(solution)/shard_map/reduce_scatter | solution.py:93
  543.4 1.6 copy-start.1
  554.1 1.2 copy-start.2
Sparse Core Ops, SparseCore 0:
  10.1 75.7 all-gather.2
  88.8 273.8 all-reduce.5
  386.9 76.5 reduce-scatter.2
  466.1 68.1 all-gather.4
  539.2 263.8 all-reduce.3
  808.4 124.9 reduce-scatter.4
where the time goes:
time: 944 us; the launch traced here: 942 us
  waiting for transfers between devices  869 us (92%)
  other arithmetic  26.9 us (3%)
  local copies, waits for them, and re-layouts  20.1 us (2%)
  between operations  14.4 us (2%)
  matrix products  11.1 us (1%)
    psum x1, waiting for transfers between devices, spread(): return lax.psum(jnp.where(mine, shard, jnp.zeros_like(shard)), axis)  272 us
    psum x1, waiting for transfers between devices, shards(): weight_full = lax.psum(weight_term, ('rows', 'rep'))  246 us
    reduce_scatter x1, waiting for transfers between devices, shards(): lax.psum_scatter(column_terms, 'rows', scatter_dimension=1, tiled=True)  129 us
    all_gather x1, waiting for transfers between devices, shards(): row_block = lax.all_gather(features, 'rep', axis=0, tiled=True)  77.9 us
    reduce_scatter x1, waiting for transfers between devices, shards(): lax.psum_scatter(partial_value.astype(jnp.bfloat16), 'rep', scatter_dimen...  76.7 us
    all_gather x1, waiting for transfers between devices, shards(): grad_rows = lax.all_gather(grad_agg, 'rep', axis=0, tiled=True)  66.4 us
  transfers between devices with their start and end apart: 6, of which 6 were waited for; matrix products, arithmetic and copies ran while one was open for 3% of the time, Pallas kernels for 0%

commit v1 on v0

v1 whole, which is shorter than its diff:
```python
import functools

import jax
import jax.numpy as jnp
from jax import lax
from jax.experimental import pallas as pl
from jax.experimental.pallas import tpu as pltpu
from jax.sharding import PartitionSpec as P

N = 8
Q = 2 * N
HALF = N // 2
TILE = 128
SLOTS = 16
NT = 2 * SLOTS
SHIFT = N
F32 = jnp.float32
BF16 = jnp.bfloat16
MESH = pl.DeviceIdType.MESH
N_SEMS = 192


class Links:
    def __init__(self, send_sems, recv_sems):
        self.send_sems, self.recv_sems, self.copies = send_sems, recv_sems, []

    def send(self, src, dst, device):
        i = len(self.copies)
        copy = pltpu.make_async_remote_copy(
            src_ref=src,
            dst_ref=dst,
            send_sem=self.send_sems.at[i],
            recv_sem=self.recv_sems.at[i],
            device_id=device,
            device_id_type=MESH,
        )
        copy.start()
        self.copies.append(copy)
        return copy

    def finish(self):
        for copy in self.copies:
            copy.wait_send()


def wait(copies):
    for copy in copies:
        copy.wait_recv()


def gather_ring(links, buf, pos, sub, right, left, partner, arrived=None):
    own, other = buf.at[pos * 2 + sub], buf.at[pos * 2 + 1 - sub]
    pair = links.send(own, own, partner)
    to_right, to_left = [links.send(own, own, right)], [links.send(own, own, left)]
    yield
    pair.wait_recv()
    to_right.append(links.send(other, other, right))
    to_left.append(links.send(other, other, left))
    if arrived:
        arrived(pos)
    yield
    for k in range(1, HALF):
        rp, lp = lax.rem(pos + N - k, N), lax.rem(pos + k, N)
        last = k == HALF - 1
        wait(to_right)
        chunk = buf.at[pl.ds(rp * 2, 1 if last else 2)]
        to_right = [links.send(chunk, chunk, right)]
        if arrived:
            arrived(rp)
        wait(to_left)
        chunk = buf.at[pl.ds(lp * 2 + 1, 1) if last else pl.ds(lp * 2, 2)]
        to_left = [links.send(chunk, chunk, left)]
        if arrived:
            arrived(lp)
        yield
    wait(to_right)
    wait(to_left)
    if arrived:
        arrived(lax.rem(pos + HALF, N))
    yield


def scatter_ring(links, own, prep, from_left, from_right, kept, pair_out, pair_in, pos, sub, right, left, partner, done):
    def add(slot, block):
        return (slot.astype(F32) + block.astype(F32)).astype(BF16)

    far = lax.rem(pos + HALF, N)
    prep(far)
    to_right = links.send(own.at[far * 2], from_left.at[0, 0], right)
    to_left = links.send(own.at[far * 2 + 1], from_right.at[0, 1], left)
    yield
    for k in range(1, HALF):
        rp, lp = lax.rem(pos + HALF - k, N), lax.rem(pos + N - HALF + k, N)
        for arriving, p, slots, device, first in (
            (to_right, rp, from_left, right, 0),
            (to_left, lp, from_right, left, 1),
        ):
            prep(p)
            arriving.wait_recv()
            if k == 1:
                slots[0, first] = add(slots[0, first], own[p * 2 + first])
                slots[0, 1 - first] = own[p * 2 + 1 - first]
            else:
                slots[k - 1, 0] = add(slots[k - 1, 0], own[p * 2])
                slots[k - 1, 1] = add(slots[k - 1, 1], own[p * 2 + 1])
            copy = links.send(slots.at[k - 1], slots.at[k], device)
            if device is right:
                to_right = copy
            else:
                to_left = copy
        yield
    prep(pos)
    wait([to_right, to_left])

    def total(s):
        value = own[pos * 2 + s].astype(F32)
        return value + from_left[HALF - 1, s].astype(F32) + from_right[HALF - 1, s].astype(F32)

    pair_out[...] = total(1 - sub).astype(BF16)
    pair = links.send(pair_out, pair_in, partner)
    kept[...] = total(sub)
    yield
    pair.wait_recv()
    done(kept[...] + pair_in[...].astype(F32))
    yield


def drain(*parts):
    parts = list(parts)
    while parts:
        for part in list(parts):
            if next(part, "end") == "end":
                parts.remove(part)


def step(part, count=1):
    for _ in range(count):
        next(part, None)


def kernel(
    feat, adj, ids, counts, weight, gout,
    act_out, gw_out, gf_out,
    fbuf0, fbuf1, gbuf0, gbuf1, part0, part1, term0, term1, xterm0, xterm1, adj_t, prod, agg, gpre,
    fl0, fr0, fl1, fr1, bl0, br0, bl1, br1, kept, pairs, kept_b, pairs_b,
    wt, wl, wr, wkept, wpair, wsum, wgather,
    kf, kb, pf, pb, lf, lb, send_sems, recv_sems,
):
    row, rep = lax.axis_index("rows"), lax.axis_index("rep")
    z, xh, core = row // 4, lax.rem(row // 2, 2), lax.rem(row, 2)
    xl, y = rep // N, lax.rem(rep, N)
    place = z * 2 + xh

    def device(z=z, xh=xh, core=core, xl=xl, y=y):
        return {"rows": (z * 2 + xh) * 2 + core, "rep": xl * N + y}

    def chip(a, b):
        return {"rows": a * 2 + core, "rep": b}

    up, down = device(z=lax.rem(z + 1, N)), device(z=lax.rem(z + N - 1, N))
    north, south = device(y=lax.rem(y + 1, N)), device(y=lax.rem(y + N - 1, N))
    far_x, near_x, sibling = device(xh=1 - xh), device(xl=1 - xl), device(core=1 - core)
    target_place = lax.rem(rep + SHIFT, Q)
    target = chip(target_place, place)
    source = chip(rep, lax.rem(place + Q - SHIFT, Q))

    barrier = pltpu.get_barrier_semaphore()
    friends = (up, down, north, south, far_x, near_x, sibling, target, source)
    for friend in friends:
        pl.semaphore_signal(barrier, inc=1, device_id=friend, device_id_type=MESH)
    pl.semaphore_wait(barrier, len(friends))

    links = Links(send_sems, recv_sems)
    fbufs, gbufs, parts, terms, xterms = (fbuf0, fbuf1), (gbuf0, gbuf1), (part0, part1), (term0, term1), (xterm0, xterm1)
    first = [
        links.send(feat.at[:, pl.ds(h * TILE, TILE)], fbufs[h].at[core, target_place], target) for h in range(2)
    ]

    @pl.loop(0, NT)
    def _(t):
        sec, i = t // SLOTS, lax.rem(t, SLOTS)
        name = ids[0, sec, i]
        live = i < counts[0, sec]
        kf[t] = jnp.where(live, lax.div(name, Q), -1 - t)
        kb[t] = jnp.where(live, lax.rem(name, Q) + sec * Q, -1 - t)

    def chains(keys, before, last, n_keys):
        @pl.loop(0, NT)
        def _(t):
            best, mine = NT, keys[t]
            for u in range(NT):
                best = jnp.where((keys[u] == mine) & (u < t), u, best)
            before[t] = best

        @pl.loop(0, n_keys)
        def _(i):
            best = NT
            for u in range(NT):
                best = jnp.where(keys[u] == i, u, best)
            last[i] = best

    chains(kf, pf, lf, Q)
    chains(kb, pb, lb, 2 * Q)
    prod[NT] = jnp.zeros((TILE, TILE), F32)

    @pl.loop(0, NT)
    def _(t):
        adj_t[t] = adj[0, t // SLOTS, lax.rem(t, SLOTS)].T

    def share(h):
        copies = []

        def arrived(p):
            chunk = fbufs[h].at[core, pl.ds(p * 2, 2)]
            copies.append(links.send(chunk, chunk, sibling))

        def run():
            first[h].wait_recv()
            yield from gather_ring(links, fbufs[h].at[core], z, xh, up, down, far_x, arrived)
            wait(copies)

        return run()

    def forward(h):
        for sec in range(2):

            @pl.loop(0, SLOTS, unroll=4)
            def _(i):
                slot = lax.rem(lax.rem(ids[0, sec, i], Q) + SHIFT, Q)
                prod[sec * SLOTS + i] = jnp.dot(adj[0, sec, i], fbufs[h][sec, slot], preferred_element_type=F32)

            yield

        @pl.loop(0, NT)
        def _(t):
            prod[t] = prod[t] + prod[pf[t]]

        for off in (4, 3, 5, 2, 6, 1, 7, 0):
            yy = lax.rem(y + off, N)
            for s in range(2):
                parts[h][yy * 2 + s] = prod[lf[s * N + yy]].astype(BF16)
        yield

    def backward(h):
        for sec in range(2):

            @pl.loop(0, SLOTS, unroll=4)
            def _(i):
                tile_row = lax.div(ids[0, sec, i], Q)
                slot = lax.rem(tile_row, N) * 2 + lax.div(tile_row, N)
                t = sec * SLOTS + i
                prod[t] = jnp.dot(adj_t[t], gbufs[h][slot], preferred_element_type=F32)

            yield

        @pl.loop(0, NT)
        def _(t):
            prod[t] = prod[t] + prod[pb[t]]

        yield

    def pair_terms(h):
        copies = {}
        for off in (4, 3, 5, 2, 6, 1, 7, 0):
            zz = lax.rem(z + off, N)
            for s in range(2):
                for sec in range(2):
                    value = prod[lb[sec * Q + zz * 2 + s]].astype(BF16)
                    for half in range(2):
                        terms[h][half, zz * 2 + s, pl.ds(sec * 64, 64)] = value[half * 64 : half * 64 + 64]
            chunk = pl.ds(zz * 2, 2)
            copies[off] = links.send(terms[h].at[1 - core, chunk], xterms[h].at[chunk], sibling)
        return copies

    share0, share1 = share(0), share(1)
    step(share0, 3)
    for _ in range(3):
        step(share0)
        step(share1)
    drain(share0)
    forward0, forward1 = forward(0), forward(1)
    step(forward0)
    step(share1)
    step(forward0)
    step(share1)
    drain(forward0)

    def sum_parts(h, slots, fin):
        return scatter_ring(
            links, parts[h], lambda p: None, *slots, kept.at[h], pairs.at[h, 0], pairs.at[h, 1], y, xl, north, south, near_x, fin
        )

    def set_agg(h):
        def fin(value):
            agg[h] = value.astype(BF16)

        return fin

    sum0 = sum_parts(0, (fl0, fr0), set_agg(0))
    step(sum0)
    drain(share1)
    step(sum0)
    step(forward1)
    step(sum0)
    step(forward1)
    step(sum0)
    drain(forward1)
    sum1 = sum_parts(1, (fl1, fr1), set_agg(1))
    step(sum1)
    drain(sum0, sum1)

    pre = jnp.dot(agg[0], weight[pl.ds(0, TILE)], preferred_element_type=F32)
    pre = pre + jnp.dot(agg[1], weight[pl.ds(TILE, TILE)], preferred_element_type=F32)
    gate = jax.nn.sigmoid(pre)
    act_out[...] = (pre * gate).astype(BF16)
    gpre[...] = (gout[...].astype(F32) * gate * (1.0 + pre * (1.0 - gate))).astype(BF16)
    own = y * 2 + xl
    for h in range(2):
        gbufs[h][own] = lax.dot_general(
            gpre[...], weight[pl.ds(h * TILE, TILE)], (((1,), (1,)), ((), ())), preferred_element_type=F32
        ).astype(BF16)
    grad0 = gather_ring(links, gbuf0, y, xl, north, south, near_x)
    grad1 = gather_ring(links, gbuf1, y, xl, north, south, near_x)
    step(grad0, 2)

    gpre_t = gpre[...].T
    rows = 2 * TILE // Q
    for h in range(2):
        value = jnp.dot(gpre_t, agg[h], preferred_element_type=F32).astype(BF16)
        for p in range(Q):
            wt[(p % N) * 2 + p // N, :, pl.ds(h * TILE, TILE)] = value[p * rows : (p + 1) * rows]

    def weight_gradient():
        def fin(value):
            wsum[0] = value

        yield from scatter_ring(
            links, wt, lambda p: None, wl, wr, wkept, wpair.at[0], wpair.at[1], y, xl, north, south, near_x, fin
        )
        pair = links.send(wsum.at[0], wsum.at[1], sibling)
        yield
        pair.wait_recv()
        wgather[place] = wsum[0] + wsum[1]
        yield from gather_ring(links, wgather, z, xh, up, down, far_x)
        value = wgather[0]
        for q in range(1, Q):
            value = value + wgather[q]
        value = jnp.concatenate([value, jnp.zeros((TILE - rows, 2 * TILE), F32)], axis=0)
        gw_out[...] = value.T[:, :rows]
        yield

    wgrad = weight_gradient()
    step(grad0)
    step(grad1, 2)
    for _ in range(3):
        step(grad0)
        step(grad1)
        step(wgrad)
    drain(grad0)
    backward0, backward1 = backward(0), backward(1)
    step(backward0)
    step(grad1)
    step(wgrad)
    step(backward0)
    drain(grad1)
    step(wgrad)
    drain(backward0)

    def sum_terms(h, slots):
        copies = pair_terms(h)

        def prep(p):
            off = [4, 3, 5, 2, 6, 1, 7, 0][len(used)]
            used.append(off)
            copies[off].wait_recv()
            for s in range(2):
                value = terms[h][core, p * 2 + s].astype(F32) + xterms[h][p * 2 + s].astype(F32)
                terms[h][core, p * 2 + s] = value.astype(BF16)

        used = []

        def fin(value):
            for sec in range(2):
                gf_out[sec, :, pl.ds(h * TILE, TILE)] = value[sec * 64 : sec * 64 + 64]

        return scatter_ring(
            links, terms[h].at[core], prep, *slots, kept_b.at[h], pairs_b.at[h, 0], pairs_b.at[h, 1], z, xh, up, down, far_x, fin
        )

    out0 = sum_terms(0, (bl0, br0))
    step(out0)
    step(backward1)
    step(wgrad)
    step(out0)
    step(backward1)
    step(out0)
    step(wgrad)
    drain(backward1)
    out1 = sum_terms(1, (bl1, br1))
    step(out1)
    drain(out0, out1, wgrad)
    links.finish()


def shards(features, adjacency, tile_ids, tile_counts, weight, grad_out):
    block = (TILE, TILE)
    vmem = pl.BlockSpec(memory_space=pltpu.VMEM)
    smem = pl.BlockSpec(memory_space=pltpu.SMEM)
    rows = 2 * TILE // Q
    slots = pltpu.VMEM((HALF, 2) + block, BF16)
    return pl.pallas_call(
        kernel,
        out_shape=(
            jax.ShapeDtypeStruct((TILE, 2 * TILE), BF16),
            jax.ShapeDtypeStruct((2 * TILE, rows), F32),
            jax.ShapeDtypeStruct((2, 64, 2 * TILE), F32),
        ),
        in_specs=[vmem, vmem, smem, smem, vmem, vmem],
        out_specs=(vmem, vmem, vmem),
        scratch_shapes=[
            pltpu.VMEM((2, Q) + block, BF16),
            pltpu.VMEM((2, Q) + block, BF16),
            pltpu.VMEM((Q,) + block, BF16),
            pltpu.VMEM((Q,) + block, BF16),
            pltpu.VMEM((Q,) + block, BF16),
            pltpu.VMEM((Q,) + block, BF16),
            pltpu.VMEM((2, Q) + block, BF16),
            pltpu.VMEM((2, Q) + block, BF16),
            pltpu.VMEM((Q,) + block, BF16),
            pltpu.VMEM((Q,) + block, BF16),
            pltpu.VMEM((NT,) + block, BF16),
            pltpu.VMEM((NT + 1,) + block, F32),
            pltpu.VMEM((2,) + block, BF16),
            pltpu.VMEM((TILE, 2 * TILE), BF16),
            *([slots] * 8),
            pltpu.VMEM((2,) + block, F32),
            pltpu.VMEM((2, 2) + block, BF16),
            pltpu.VMEM((2,) + block, F32),
            pltpu.VMEM((2, 2) + block, BF16),
            pltpu.VMEM((Q, rows, 2 * TILE), BF16),
            pltpu.VMEM((HALF, 2, rows, 2 * TILE), BF16),
            pltpu.VMEM((HALF, 2, rows, 2 * TILE), BF16),
            pltpu.VMEM((rows, 2 * TILE), F32),
            pltpu.VMEM((2, rows, 2 * TILE), BF16),
            pltpu.VMEM((2, rows, 2 * TILE), F32),
            pltpu.VMEM((Q, rows, 2 * TILE), F32),
            pltpu.SMEM((NT,), jnp.int32),
            pltpu.SMEM((NT,), jnp.int32),
            pltpu.SMEM((NT,), jnp.int32),
            pltpu.SMEM((NT,), jnp.int32),
            pltpu.SMEM((Q,), jnp.int32),
            pltpu.SMEM((2 * Q,), jnp.int32),
            pltpu.SemaphoreType.DMA((N_SEMS,)),
            pltpu.SemaphoreType.DMA((N_SEMS,)),
        ],
        compiler_params=pltpu.CompilerParams(
            collective_id=0, has_side_effects=True, vmem_limit_bytes=40 * 1024 * 1024
        ),
    )(features, adjacency, tile_ids, tile_counts, weight, grad_out)


def solution(mesh):
    return jax.shard_map(
        shards,
        mesh=mesh,
        in_specs=(
            P(("rows", "rep"), None),
            P("rows", "rep", None, None, None),
            P("rows", "rep", None),
            P("rows", "rep"),
            P(),
            P(("rows", "rep"), None),
        ),
        out_specs=(P(("rows", "rep"), None), P(None, "rep"), P("rep", "rows", None)),
        check_vma=False,
    )
```

time: 944 us -> 150 us (0.16)
  waiting for transfers between devices: 869 us -> 0 us
  Pallas kernels: 0 us -> 142 us
  other arithmetic: 26.9 us -> 0 us
  between operations: 14.4 us -> 0.65 us
  local copies, waits for them, and re-layouts: 20.1 us -> 7.09 us
  matrix products: 11.1 us -> 0 us
    psum x2 -> x0, waiting for transfers between devices: 518 us -> none  [the longest x1 272 us: spread(): return lax.psum(jnp.where(mine, shard, jnp.zeros_like(shard)), axis)]
    reduce_scatter x2 -> x0, waiting for transfers between devices: 206 us -> none  [the longest x1 129 us: shards(): lax.psum_scatter(column_terms, 'rows', scatter_dimension=1, tiled=True)]
    all_gather x2 -> x0, waiting for transfers between devices: 144 us -> none  [the longest x1 77.9 us: shards(): row_block = lax.all_gather(features, 'rep', axis=0, tiled=True)]
    pallas_call x0 -> x1, Pallas kernels: none -> 142 us  [shards(): pl.pallas_call(kernel, out_shape=(jax.ShapeDtypeStruct((TILE, 2 * TILE),...]
    scatter-add x4 -> x0, other arithmetic: 15.8 us -> none  [place_rows(): placed = jnp.zeros((tiles_per, product.shape[1], product.shape[2]), jnp.f...]
    dot_general x7 -> x0, matrix products: 11.1 us -> none  [the longest x2 3.55 us: backward_tiles(): jnp.einsum('tji,tjf->tif', tile_block, picked, preferred_element_type=jnp...]
  transfers between devices with their start and end apart: 6 -> 0, of which waited for: 6 -> 0; matrix products, arithmetic and copies ran while one was open for 3% -> 0% of each run, Pallas kernels for 0% -> 0%
where the time goes in v1:
time: 150 us
  Pallas kernels  142 us (95%)
  local copies, waits for them, and re-layouts  7.09 us (5%)
    pallas_call x1, Pallas kernels, shards(): pl.pallas_call(kernel, out_shape=(jax.ShapeDtypeStruct((TILE, 2 * TILE),...  142 us
    unnamed x14, local copies, waits for them, and re-layouts  6.42 us

profile of v1, /device:TPU:6, one launch (start us, length us, event | category | flops | bytes accessed | tf_op | source)
XLA Modules:
  0.0 149.5 jit_solution(8808291002694643127)
XLA Ops:
  0.6 0.0 copy-start
  0.6 1.2 copy-done
  1.9 0.0 copy-start.1
  1.9 0.9 copy-done.1
  2.8 0.0 copy-start.2
  2.8 0.8 copy-done.2
  3.6 0.0 copy-start.3
  3.6 0.8 copy-done.3
  4.4 0.0 copy-start.4
  4.4 0.7 copy-done.4
  5.1 0.0 copy-start.5
  5.1 0.7 copy-done.5
  5.8 141.8 %shard_map.85 = (bf16[128,256]{1,0:T(8,128)(2,1)S(1)}, f32[256,16]{1,0:T(8,128)S(1)}, f32[2,64,256]{2,1,0:T(8,128)S(1)}) custom-call(bf16[128,256]{1,0:T(8,128)(2,1)S(1)} %copy-done.2, bf16[1,2,16,128,128]{4,3,2,1,0:T(8,128)(2,1)S(1)} %copy-done, s32[1,2,16]{2,1,0:T(2,128)S(1)} %copy-done.4, s32[1,2]{1,0:T(1,128)S(1)} %copy-done.5, ...), custom_call_target="tpu_custom_call" | custom-call | tf_op jit(solution)/shard_map/pallas_call | solution.py:411
  147.6 0.7 copy.9
  148.3 0.6 copy.12
  148.9 0.7 copy.13
Async XLA Ops:
  0.6 1.2 copy-start
  1.9 0.9 copy-start.1
  2.8 0.8 copy-start.2
  3.6 0.8 copy-start.3
  4.4 0.7 copy-start.4
  5.1 0.7 copy-start.5

commit v2 on v1

v2 whole, which is shorter than its diff:
```python
import jax
import jax.numpy as jnp
from jax import lax
from jax.experimental import pallas as pl
from jax.experimental.pallas import tpu as pltpu
from jax.sharding import PartitionSpec as P

N = 8
Q = 2 * N
HALF = N // 2
TILE = 128
SLOTS = 16
NT = 2 * SLOTS
OFFSETS = (4, 3, 5, 2, 6, 1, 7, 0)
F32 = jnp.float32
BF16 = jnp.bfloat16
MESH = pl.DeviceIdType.MESH
N_SEMS = 185


class Links:
    def __init__(self, send_sems, recv_sems):
        self.send_sems, self.recv_sems, self.copies = send_sems, recv_sems, []

    def send(self, src, dst, device):
        i = len(self.copies)
        assert i < N_SEMS
        copy = pltpu.make_async_remote_copy(
            src_ref=src,
            dst_ref=dst,
            send_sem=self.send_sems.at[i],
            recv_sem=self.recv_sems.at[i],
            device_id=device,
            device_id_type=MESH,
        )
        copy.start()
        self.copies.append(copy)
        return copy

    def finish(self):
        for copy in self.copies:
            copy.wait_send()


def wait(copies):
    for copy in copies:
        copy.wait_recv()


def gather_ring(links, buf, pos, sub, ways, partner, arrived=None):
    own = buf.at[pos * 2 + sub]
    pending = []
    for near, across in ways:
        pending.append([links.send(own, own, near), links.send(own, own, across)])
    pair = links.send(own, own, partner)
    yield
    for k in range(1, HALF):
        for side in range(2):
            p = lax.rem(pos + (N - k, k)[side], N)
            moved = []
            for s in range(2):
                pending[side][s].wait_recv()
                if k < HALF - 1 or s == side:
                    block = buf.at[p * 2 + (sub if s == 0 else 1 - sub)]
                    moved.append(links.send(block, block, ways[side][0]))
            pending[side] = moved
            if arrived:
                arrived(p)
        if k == 1:
            pair.wait_recv()
            if arrived:
                arrived(pos)
        yield
    wait(pending[0] + pending[1])
    if arrived:
        arrived(lax.rem(pos + HALF, N))
    yield


def scatter_ring(links, own, prep, slots, last, pos, sub, ways, partner, done):
    def add(slot, block):
        return (slot.astype(F32) + block.astype(F32)).astype(BF16)

    far = lax.rem(pos + HALF, N)
    prep(far)
    pending = [[links.send(own.at[far * 2 + side], slots.at[side, 0, side], ways[side][0])] for side in range(2)]
    yield
    ending = []
    for k in range(1, HALF):
        for side in range(2):
            p = lax.rem(pos + (HALF - k, N - HALF + k)[side], N)
            prep(p)
            moved = []
            for s in range(2):
                here = slots.at[side, k - 1, s]
                if k == 1 and s != side:
                    here = own.at[p * 2 + s]
                else:
                    pending[side][0 if k == 1 else s].wait_recv()
                    here[...] = add(here[...], own[p * 2 + s])
                if k < HALF - 1:
                    moved.append(links.send(here, slots.at[side, k, s], ways[side][0]))
            if k == HALF - 1:
                for t in range(2):
                    block = slots.at[side, k - 1, sub if t == 0 else 1 - sub]
                    ending.append(links.send(block, last.at[side * 2 + t], ways[side][t]))
            pending[side] = moved
        if k == HALF - 1:
            prep(pos)
            ending.append(links.send(own.at[pos * 2 + 1 - sub], last.at[4], partner))
        yield
    wait(ending)
    value = own[pos * 2 + sub].astype(F32)
    for i in range(5):
        value = value + last[i].astype(F32)
    done(value)
    yield


def drain(*parts):
    parts = list(parts)
    while parts:
        for part in list(parts):
            if next(part, "end") == "end":
                parts.remove(part)


def step(part, count=1):
    for _ in range(count):
        next(part, None)


def kernel(
    feat_in, adj_in, ids_in, counts_in, weight_in, gout_in,
    act_out, gw_out, gf_out,
    feat, adj, weight, gout, fbuf0, fbuf1, gbuf0, gbuf1, part0, part1, term0, term1, xterm0, xterm1, adj_t, prod, agg, gpre,
    fslots0, fslots1, flast0, flast1, bslots0, bslots1, blast0, blast1,
    wt, wslots, wlast, wsum, wgather,
    ids, counts, kf, kb, pf, pb, lf, lb, local_sems, send_sems, recv_sems,
):
    row, rep = lax.axis_index("rows"), lax.axis_index("rep")
    z, xh, core = row // 4, lax.rem(row // 2, 2), lax.rem(row, 2)
    xl, y = rep // N, lax.rem(rep, N)
    place = z * 2 + xh

    loads = [
        pltpu.make_async_copy(src, dst, local_sems.at[i])
        for i, (src, dst) in enumerate(
            [(feat_in.at[:, pl.ds(h * TILE, TILE)], feat.at[h]) for h in range(2)]
            + [(ids_in, ids), (counts_in, counts), (adj_in, adj), (weight_in, weight), (gout_in, gout)]
        )
    ]
    for load in loads:
        load.start()

    def device(z=z, xh=xh, core=core, xl=xl, y=y):
        return {"rows": (z * 2 + xh) * 2 + core, "rep": xl * N + y}

    def turn(value, by):
        return lax.rem(value + by + 2 * N, N)

    up, down = turn(z, 1), turn(z, -1)
    north, south = turn(y, 1), turn(y, -1)
    z_ways = [(device(z=t), device(z=t, xh=1 - xh)) for t in (up, down)]
    y_ways = [(device(y=t), device(y=t, xl=1 - xl)) for t in (north, south)]
    far_x, near_x, sibling = device(xh=1 - xh), device(xl=1 - xl), device(core=1 - core)

    def entry(z, xh, xl, y):
        home = z * 2 + xh
        return turn(z, y - lax.rem(home, N) + HALF), lax.rem(xl + home // N + xh, 2)

    tz, txh = entry(z, xh, xl, y)
    target = device(z=tz, xh=txh, xl=place // N, y=lax.rem(place, N))
    sz, sxh = rep // 2, lax.rem(rep, 2)
    source = device(z=sz, xh=sxh, xl=lax.rem(xh + xl + sxh, 2), y=turn(z, y - sz - HALF))

    barrier = pltpu.get_barrier_semaphore()
    friends = (*z_ways[0], *z_ways[1], *y_ways[0], *y_ways[1], far_x, near_x, sibling, target, source)
    for friend in friends:
        pl.semaphore_signal(barrier, inc=1, device_id=friend, device_id_type=MESH)
    pl.semaphore_wait(barrier, len(friends))

    links = Links(send_sems, recv_sems)
    fbufs, gbufs, parts, terms, xterms = (fbuf0, fbuf1), (gbuf0, gbuf1), (part0, part1), (term0, term1), (xterm0, xterm1)
    first = []
    for h in range(2):
        loads[h].wait()
        first.append(links.send(feat.at[h], fbufs[h].at[core, tz * 2 + txh], target))
    for load in loads[2:]:
        load.wait()

    @pl.loop(0, NT)
    def _(t):
        sec, i = t // SLOTS, lax.rem(t, SLOTS)
        name = ids[0, sec, i]
        live = i < counts[0, sec]
        kf[t] = jnp.where(live, lax.div(name, Q), -1 - t)
        kb[t] = jnp.where(live, lax.rem(name, Q) + sec * Q, -1 - t)

    def chains(keys, before, last, n_keys):
        @pl.loop(0, NT)
        def _(t):
            best, mine = NT, keys[t]
            for u in range(NT):
                best = jnp.where((keys[u] == mine) & (u < t), u, best)
            before[t] = best

        @pl.loop(0, n_keys)
        def _(i):
            best = NT
            for u in range(NT):
                best = jnp.where(keys[u] == i, u, best)
            last[i] = best

    def transpose(sec):
        @pl.loop(0, SLOTS)
        def _(i):
            adj_t[sec * SLOTS + i] = adj[0, sec, i].T

    def share(h):
        copies = []

        def arrived(p):
            chunk = fbufs[h].at[core, pl.ds(p * 2, 2)]
            copies.append(links.send(chunk, chunk, sibling))

        def run():
            first[h].wait_recv()
            yield from gather_ring(links, fbufs[h].at[core], z, xh, z_ways, far_x, arrived)
            wait(copies)

        return run()

    def forward(h):
        for sec in range(2):

            @pl.loop(0, SLOTS, unroll=4)
            def _(i):
                column = lax.rem(ids[0, sec, i], Q)
                ez, exh = entry(sz, sxh, column // N, lax.rem(column, N))
                prod[sec * SLOTS + i] = jnp.dot(adj[0, sec, i], fbufs[h][sec, ez * 2 + exh], preferred_element_type=F32)

            yield

        @pl.loop(0, NT)
        def _(t):
            prod[t] = prod[t] + prod[pf[t]]

        for off in OFFSETS:
            yy = turn(y, off)
            for s in range(2):
                parts[h][yy * 2 + s] = prod[lf[s * N + yy]].astype(BF16)
        yield

    def backward(h):
        for sec in range(2):

            @pl.loop(0, SLOTS, unroll=4)
            def _(i):
                tile_row = lax.div(ids[0, sec, i], Q)
                slot = lax.rem(tile_row, N) * 2 + lax.div(tile_row, N)
                t = sec * SLOTS + i
                prod[t] = jnp.dot(adj_t[t], gbufs[h][slot], preferred_element_type=F32)

            yield

        @pl.loop(0, NT)
        def _(t):
            prod[t] = prod[t] + prod[pb[t]]

        yield

    def pair_terms(h):
        copies = {}
        for off in OFFSETS:
            zz = turn(z, off)
            for s in range(2):
                for sec in range(2):
                    value = prod[lb[sec * Q + zz * 2 + s]].astype(BF16)
                    for half in range(2):
                        terms[h][half, zz * 2 + s, pl.ds(sec * 64, 64)] = value[half * 64 : half * 64 + 64]
            chunk = pl.ds(zz * 2, 2)
            copies[off] = links.send(terms[h].at[1 - core, chunk], xterms[h].at[chunk], sibling)
        return copies

    chains(kf, pf, lf, Q)
    prod[NT] = jnp.zeros((TILE, TILE), F32)
    share0, share1 = share(0), share(1)
    step(share0)
    step(share1)
    chains(kb, pb, lb, 2 * Q)
    step(share0)
    step(share1)
    transpose(0)
    step(share0)
    step(share1)
    transpose(1)
    step(share0)
    step(share1)
    step(share0)
    step(share1)
    drain(share0)

    def sum_parts(h, slots, last):
        def fin(value):
            agg[h] = value.astype(BF16)

        return scatter_ring(links, parts[h], lambda p: None, slots, last, y, xl, y_ways, near_x, fin)

    drain(forward(0))
    sum0 = sum_parts(0, fslots0, flast0)
    step(sum0)
    drain(share1)
    drain(forward(1))
    sum1 = sum_parts(1, fslots1, flast1)
    step(sum1)
    drain(sum0, sum1)

    pre = jnp.dot(agg[0], weight[pl.ds(0, TILE)], preferred_element_type=F32)
    pre = pre + jnp.dot(agg[1], weight[pl.ds(TILE, TILE)], preferred_element_type=F32)
    gate = jax.nn.sigmoid(pre)
    act_out[...] = (pre * gate).astype(BF16)
    gpre[...] = (gout[...].astype(F32) * gate * (1.0 + pre * (1.0 - gate))).astype(BF16)
    own = y * 2 + xl
    grads = []
    for h in range(2):
        gbufs[h][own] = lax.dot_general(
            gpre[...], weight[pl.ds(h * TILE, TILE)], (((1,), (1,)), ((), ())), preferred_element_type=F32
        ).astype(BF16)
        grads.append(gather_ring(links, gbufs[h], y, xl, y_ways, near_x))
        step(grads[h])

    gpre_t = gpre[...].T
    rows = 2 * TILE // Q
    for h in range(2):
        value = jnp.dot(gpre_t, agg[h], preferred_element_type=F32).astype(BF16)
        for p in range(Q):
            wt[(p % N) * 2 + p // N, :, pl.ds(h * TILE, TILE)] = value[p * rows : (p + 1) * rows]

    def weight_gradient():
        def fin(value):
            wsum[0] = value

        yield from scatter_ring(links, wt, lambda p: None, wslots, wlast, y, xl, y_ways, near_x, fin)
        pair = links.send(wsum.at[0], wsum.at[1], sibling)
        yield
        pair.wait_recv()
        wgather[place] = wsum[0] + wsum[1]
        yield from gather_ring(links, wgather, z, xh, z_ways, far_x)
        value = wgather[0]
        for q in range(1, Q):
            value = value + wgather[q]
        gw_out[...] = value
        yield

    wgrad = weight_gradient()
    step(wgrad)
    for _ in range(3):
        step(grads[0])
        step(grads[1])
        step(wgrad)
    drain(grads[0])
    backward0, backward1 = backward(0), backward(1)
    step(backward0)
    drain(grads[1])
    step(wgrad)
    drain(backward0)

    def sum_terms(h, copies, slots, last):
        order = iter(OFFSETS)

        def prep(p):
            copies[next(order)].wait_recv()
            for s in range(2):
                value = terms[h][core, p * 2 + s].astype(F32) + xterms[h][p * 2 + s].astype(F32)
                terms[h][core, p * 2 + s] = value.astype(BF16)

        def fin(value):
            for sec in range(2):
                gf_out[sec, :, pl.ds(h * TILE, TILE)] = value[sec * 64 : sec * 64 + 64]

        return scatter_ring(links, terms[h].at[core], prep, slots, last, z, xh, z_ways, far_x, fin)

    out0 = sum_terms(0, pair_terms(0), bslots0, blast0)
    step(backward1)
    step(out0)
    step(wgrad)
    drain(backward1)
    out1 = sum_terms(1, pair_terms(1), bslots1, blast1)
    step(out0)
    step(out1)
    step(wgrad)
    drain(out0, out1, wgrad)
    links.finish()


def shards(features, adjacency, tile_ids, tile_counts, weight, grad_out):
    block = (TILE, TILE)
    hbm = pl.BlockSpec(memory_space=pltpu.HBM)
    vmem = pl.BlockSpec(memory_space=pltpu.VMEM)
    rows = 2 * TILE // Q
    stripe = (rows, 2 * TILE)
    slots, last = (2, HALF - 1, 2), (5,)
    activated, grad_weight, grad_features = pl.pallas_call(
        kernel,
        out_shape=(
            jax.ShapeDtypeStruct((TILE, 2 * TILE), BF16),
            jax.ShapeDtypeStruct(stripe, F32),
            jax.ShapeDtypeStruct((2, 64, 2 * TILE), F32),
        ),
        in_specs=[hbm] * 6,
        out_specs=(vmem, vmem, vmem),
        scratch_shapes=[
            pltpu.VMEM((2,) + block, BF16),
            pltpu.VMEM((1, 2, SLOTS) + block, BF16),
            pltpu.VMEM((2 * TILE, 2 * TILE), BF16),
            pltpu.VMEM((TILE, 2 * TILE), BF16),
            *[pltpu.VMEM((2, Q) + block, BF16)] * 2,
            *[pltpu.VMEM((Q,) + block, BF16)] * 2,
            *[pltpu.VMEM((Q,) + block, BF16)] * 2,
            *[pltpu.VMEM((2, Q) + block, BF16)] * 2,
            *[pltpu.VMEM((Q,) + block, BF16)] * 2,
            pltpu.VMEM((NT,) + block, BF16),
            pltpu.VMEM((NT + 1,) + block, F32),
            pltpu.VMEM((2,) + block, BF16),
            pltpu.VMEM((TILE, 2 * TILE), BF16),
            *[pltpu.VMEM(slots + block, BF16)] * 2,
            *[pltpu.VMEM(last + block, BF16)] * 2,
            *[pltpu.VMEM(slots + block, BF16)] * 2,
            *[pltpu.VMEM(last + block, BF16)] * 2,
            pltpu.VMEM((Q,) + stripe, BF16),
            pltpu.VMEM(slots + stripe, BF16),
            pltpu.VMEM(last + stripe, BF16),
            pltpu.VMEM((2,) + stripe, F32),
            pltpu.VMEM((Q,) + stripe, F32),
            pltpu.SMEM((1, 2, SLOTS), jnp.int32),
            pltpu.SMEM((1, 2), jnp.int32),
            pltpu.SMEM((NT,), jnp.int32),
            pltpu.SMEM((NT,), jnp.int32),
            pltpu.SMEM((NT,), jnp.int32),
            pltpu.SMEM((NT,), jnp.int32),
            pltpu.SMEM((Q,), jnp.int32),
            pltpu.SMEM((2 * Q,), jnp.int32),
            pltpu.SemaphoreType.DMA((7,)),
            pltpu.SemaphoreType.DMA((N_SEMS,)),
            pltpu.SemaphoreType.DMA((N_SEMS,)),
        ],
        compiler_params=pltpu.CompilerParams(
            collective_id=0, has_side_effects=True, vmem_limit_bytes=63 * 1024 * 1024
        ),
    )(features, adjacency, tile_ids, tile_counts, weight, grad_out)
    return activated, grad_weight.T, grad_features


def solution(mesh):
    return jax.shard_map(
        shards,
        mesh=mesh,
        in_specs=(
            P(("rows", "rep"), None),
            P("rows", "rep", None, None, None),
            P("rows", "rep", None),
            P("rows", "rep"),
            P(),
            P(("rows", "rep"), None),
        ),
        out_specs=(P(("rows", "rep"), None), P(None, "rep"), P("rep", "rows", None)),
        check_vma=False,
    )
```

time: 150 us -> 110 us (0.73)
  Pallas kernels: 142 us -> 105 us
  local copies, waits for them, and re-layouts: 7.09 us -> 3.49 us
    pallas_call x1, Pallas kernels: 142 us -> 105 us  [shards(): pl.pallas_call(kernel, out_shape=(jax.ShapeDtypeStruct((TILE, 2 * TILE),...]
    unnamed x14 -> x5, local copies, waits for them, and re-layouts: 6.42 us -> 3.49 us
where the time goes in v2:
time: 110 us
  Pallas kernels  105 us (95%)
  local copies, waits for them, and re-layouts  3.49 us (3%)
    pallas_call x1, Pallas kernels, shards(): pl.pallas_call(kernel, out_shape=(jax.ShapeDtypeStruct((TILE, 2 * TILE),...  105 us
    unnamed x5, local copies, waits for them, and re-layouts  3.49 us

profile of v2, /device:TPU:6, one launch (start us, length us, event | category | flops | bytes accessed | tf_op | source)
XLA Modules:
  0.0 109.6 jit_solution(6132058304526522722)
XLA Ops:
  0.6 105.4 %shard_map.85 = (bf16[128,256]{1,0:T(8,128)(2,1)}, f32[16,256]{1,0:T(8,128)}, f32[2,64,256]{2,1,0:T(8,128)}) custom-call(bf16[128,256]{1,0:T(8,128)(2,1)} %feat_in.1, bf16[1,2,16,128,128]{4,3,2,1,0:T(8,128)(2,1)} %adj_in.1, s32[1,2,16]{2,1,0:T(2,128)} %ids_in.1, s32[1,2]{1,0:T(1,128)} %counts_in.1, bf16[256,256]{1,0:T(8,128)(2,1)} %weight_in.1, ...), custom_call_target="tpu_custom_call" | custom-call | tf_op jit(solution)/shard_map/pallas_call | solution.py:404
  106.1 0.0 copy-start
  106.1 1.5 %copy.12 = bf16[128,256]{1,0:T(8,128)(2,1)} copy(bf16[128,256]{1,0:T(8,128)(2,1)} %get-tuple-element.12) | data formatting | bytes 131072
  107.6 1.3 %copy.13 = f32[256,16]{0,1:T(8,128)} copy(f32[256,16]{0,1:T(8,128)} %bitcast.1) | data formatting | bytes 32768
  108.9 0.0 copy-done
  108.9 0.7 copy.14
Async XLA Ops:
  106.1 2.8 %copy-start = (f32[2,64,256]{2,1,0:T(8,128)S(1)}, f32[2,64,256]{2,1,0:T(8,128)}, u32[]{:S(2)}) copy-start(f32[2,64,256]{2,1,0:T(8,128)} %get-tuple-element.14) | copy-start | bytes 393220

commit v3 on v2

v3 whole, which is shorter than its diff:
```python
import jax
import jax.numpy as jnp
from jax import lax
from jax.experimental import pallas as pl
from jax.experimental.pallas import tpu as pltpu
from jax.sharding import PartitionSpec as P

N = 8
Q = 2 * N
HALF = N // 2
TILE = 128
SLOTS = 16
NT = 2 * SLOTS
OFFSETS = (4, 3, 5, 1, 7, 0, 2, 6)
F32 = jnp.float32
BF16 = jnp.bfloat16
MESH = pl.DeviceIdType.MESH
N_SEND = 16
N_RECV = 80


class Links:
    def __init__(self, send_sems, recv_sems):
        self.send_sems, self.recv_sems, self.n_send, self.n_recv = send_sems, recv_sems, 0, 0
        self.finishing = []

    def batch(self, everything):
        sem = self.send_sems.at[self.n_send]
        self.n_send += 1
        assert self.n_send <= N_SEND
        self.finishing.append((everything, sem))
        return sem

    def arrival(self):
        sem = self.recv_sems.at[self.n_recv]
        self.n_recv += 1
        assert self.n_recv <= N_RECV
        return sem

    def send(self, src, dst, device, batch, arrival=None):
        copy = pltpu.make_async_remote_copy(
            src_ref=src,
            dst_ref=dst,
            send_sem=batch,
            recv_sem=self.arrival() if arrival is None else arrival,
            device_id=device,
            device_id_type=MESH,
        )
        copy.start()
        return copy

    def finish(self):
        for everything, sem in self.finishing:
            await_bytes(everything, sem)


def await_bytes(ref, sem):
    pltpu.make_async_copy(ref, ref, sem).wait()


def gather_ring(links, buf, pos, sub, ways, partner, arrived=None):
    own = buf.at[pos * 2 + sub]
    batch = links.batch(buf.at[pl.ds(0, Q - 1)])
    far = [[links.send(own, own, device, batch) for device in ways[1][side]] for side in range(2)]
    close = [links.arrival() for _ in range(2)]
    for side in range(2):
        for device in ways[0][side]:
            links.send(own, own, device, batch, close[side])
    pair = links.send(own, own, partner, batch)
    yield
    three, four = [links.arrival() for _ in range(2)], links.arrival()
    for side in range(2):
        p = lax.rem(pos + (N - 2, 2)[side], N)
        for s in range(2):
            far[side][s].wait_recv()
            block = buf.at[p * 2 + (sub if s == 0 else 1 - sub)]
            if s == side:
                links.send(block, block, ways[1][side][0], batch, four)
            links.send(block, block, ways[0][side][0], batch, three[side])
    if arrived:
        for side in range(2):
            arrived(lax.rem(pos + (N - 2, 2)[side], N))
    yield
    two = buf.at[pl.ds(0, 2)]
    pair.wait_recv()
    if arrived:
        arrived(pos)
    for side in range(2):
        await_bytes(two, close[side])
        if arrived:
            arrived(lax.rem(pos + (N - 1, 1)[side], N))
    yield
    for side in range(2):
        await_bytes(two, three[side])
        if arrived:
            arrived(lax.rem(pos + (N - 3, 3)[side], N))
    await_bytes(two, four)
    if arrived:
        arrived(lax.rem(pos + HALF, N))
    yield


def scatter_ring(links, own, prep, middle, last, pos, sub, ways, partner, done):
    batch, end = links.batch(own.at[pl.ds(0, Q - 1)]), links.arrival()
    halfway = [links.arrival() for _ in range(2)]

    def at(side, distance):
        return lax.rem(pos + (distance, N - distance)[side], N)

    p = at(0, HALF)
    prep(p)
    for side in range(2):
        links.send(own.at[p * 2 + side], middle.at[side, 2], ways[1][side][0], batch, halfway[side])
    for side in range(2):
        p = at(side, 3)
        prep(p)
        links.send(own.at[pl.ds(p * 2, 2)], middle.at[side, pl.ds(0, 2)], ways[0][side][0], batch, halfway[side])
    yield
    for side in range(2):
        p = at(side, 1)
        prep(p)
        for t in range(2):
            block = own.at[p * 2 + (sub if t == 0 else 1 - sub)]
            links.send(block, last.at[side * 4 + t], ways[0][side][t], batch, end)
    prep(pos)
    links.send(own.at[pos * 2 + 1 - sub], last.at[8], partner, batch, end)
    yield
    for side in range(2):
        p = at(side, 2)
        prep(p)
        await_bytes(middle.at[side], halfway[side])
        for s in range(2):
            value = middle[side, s].astype(F32) + own[p * 2 + s].astype(F32)
            if s == side:
                value = value + middle[side, 2].astype(F32)
            middle[side, s] = value.astype(BF16)
        for t in range(2):
            block = middle.at[side, sub if t == 0 else 1 - sub]
            links.send(block, last.at[side * 4 + 2 + t], ways[1][side][t], batch, end)
    yield
    await_bytes(last, end)
    value = own[pos * 2 + sub].astype(F32)
    for i in range(9):
        value = value + last[i].astype(F32)
    done(value)
    yield


def drain(*parts):
    parts = list(parts)
    while parts:
        for part in list(parts):
            if next(part, "end") == "end":
                parts.remove(part)


def step(part, count=1):
    for _ in range(count):
        next(part, None)


def kernel(
    feat_in, adj_in, ids_in, counts_in, weight_in, gout_in,
    act_out, gw_out, gf_out,
    feat, adj, weight, gout, fown0, fown1, fpair0, fpair1, gbuf0, gbuf1, part0, part1, term0, term1, xterm0, xterm1, adj_t, prod, agg, gpre,
    fslots0, fslots1, flast0, flast1, bslots0, bslots1, blast0, blast1,
    wt, wslots, wlast, wsum, wgather,
    ids, counts, table, chains, local_sems, send_sems, recv_sems,
):
    row, rep = lax.axis_index("rows"), lax.axis_index("rep")
    z, xh, core = row // 4, lax.rem(row // 2, 2), lax.rem(row, 2)
    xl, y = rep // N, lax.rem(rep, N)
    place = z * 2 + xh

    loads = [
        pltpu.make_async_copy(src, dst, local_sems.at[i])
        for i, (src, dst) in enumerate(
            [(feat_in.at[:, pl.ds(h * TILE, TILE)], feat.at[h]) for h in range(2)]
            + [(ids_in, ids), (counts_in, counts), (adj_in, adj), (weight_in, weight), (gout_in, gout)]
        )
    ]
    for load in loads:
        load.start()

    def device(z=z, xh=xh, core=core, xl=xl, y=y):
        return {"rows": (z * 2 + xh) * 2 + core, "rep": xl * N + y}

    def turn(value, by):
        return lax.rem(value + by + 2 * N, N)

    z_ways, y_ways = [], []
    for by in (1, 2):
        z_ways.append([(device(z=t), device(z=t, xh=1 - xh)) for t in (turn(z, by), turn(z, -by))])
        y_ways.append([(device(y=t), device(y=t, xl=1 - xl)) for t in (turn(y, by), turn(y, -by))])
    far_x, near_x, sibling = device(xh=1 - xh), device(xl=1 - xl), device(core=1 - core)

    def entry(z, xh, xl, y):
        home = z * 2 + xh
        return turn(z, y - lax.rem(home, N) + HALF), lax.rem(xl + home // N + xh, 2)

    tz, txh = entry(z, xh, xl, y)
    target = device(z=tz, xh=txh, xl=place // N, y=lax.rem(place, N))
    sz, sxh = rep // 2, lax.rem(rep, 2)
    source = device(z=sz, xh=sxh, xl=lax.rem(xh + xl + sxh, 2), y=turn(z, y - sz - HALF))

    barrier = pltpu.get_barrier_semaphore()
    friends = [d for ways in (z_ways, y_ways) for sides in ways for side in sides for d in side]
    friends += [far_x, near_x, sibling, target, source]
    for friend in friends:
        pl.semaphore_signal(barrier, inc=1, device_id=friend, device_id_type=MESH)
    pl.semaphore_wait(barrier, len(friends))

    links = Links(send_sems, recv_sems)
    fowns, fpairs, gbufs, parts = (fown0, fown1), (fpair0, fpair1), (gbuf0, gbuf1), (part0, part1)
    terms, xterms = (term0, term1), (xterm0, xterm1)
    batch = links.batch(feat)
    first = []
    for h in range(2):
        loads[h].wait()
        first.append(links.send(feat.at[h], fowns[h].at[tz * 2 + txh], target, batch))
    for load in loads[2:]:
        load.wait()

    along = [lax.broadcasted_iota(jnp.int32, (NT, TILE), d) for d in range(2)]

    def keys(t):
        name = jnp.zeros((NT, TILE), jnp.int32)
        for i in range(NT):
            name = jnp.where(t == i, ids[0, i // SLOTS, i % SLOTS], name)
        second = t >= SLOTS
        live = t < jnp.where(second, counts[0, 1] + SLOTS, counts[0, 0])
        by_row = jnp.where(live, lax.shift_right_logical(name, 4), -1 - t)
        by_column = jnp.where(live, (name & (Q - 1)) + jnp.where(second, Q, 0), -1 - t)
        return by_row, by_column

    def latest(which):
        t = jnp.max(jnp.where(which, along[0], -1), axis=0, keepdims=True)
        return jnp.where(t < 0, NT, t)

    table_row = lax.broadcasted_iota(jnp.int32, (8, TILE), 0)
    found = jnp.zeros((8, TILE), jnp.int32)
    for i, (down_key, across_key) in enumerate(zip(keys(along[0]), keys(along[1]))):
        before = latest((down_key == across_key) & (along[0] < along[1]))
        found = jnp.where(table_row == 2 * i, before, found)
        found = jnp.where(table_row == 2 * i + 1, latest(down_key == along[1]), found)
    table[...] = found
    chained = pltpu.make_async_copy(table, chains, local_sems.at[7])
    chained.start()

    def transpose(sec):
        @pl.loop(0, SLOTS, unroll=4)
        def _(i):
            adj_t[sec * SLOTS + i] = adj[0, sec, i].T

    def share(h):
        end = links.arrival()
        batch = links.batch(fowns[h])

        def arrived(p):
            chunk = pl.ds(p * 2, 2)
            links.send(fowns[h].at[chunk], fpairs[h].at[chunk], sibling, batch, end)

        def run():
            first[h].wait_recv()
            yield from gather_ring(links, fowns[h], z, xh, z_ways, far_x, arrived)
            await_bytes(fpairs[h], end)
            yield

        return run()

    def forward(h):
        for buf, sec in ((fowns[h], core), (fpairs[h], 1 - core)):

            @pl.loop(0, SLOTS, unroll=4)
            def _(i):
                column = lax.rem(ids[0, sec, i], Q)
                ez, exh = entry(sz, sxh, column // N, lax.rem(column, N))
                prod[sec * SLOTS + i] = jnp.dot(adj[0, sec, i], buf[ez * 2 + exh], preferred_element_type=F32)

            yield

        @pl.loop(0, NT, unroll=2)
        def _(t):
            prod[t] = prod[t] + prod[chains[0, t]]

        for off in OFFSETS:
            yy = turn(y, off)
            for s in range(2):
                parts[h][yy * 2 + s] = prod[chains[1, s * N + yy]].astype(BF16)
        yield

    def backward(h):
        for sec in range(2):

            @pl.loop(0, SLOTS, unroll=4)
            def _(i):
                tile_row = lax.div(ids[0, sec, i], Q)
                slot = lax.rem(tile_row, N) * 2 + lax.div(tile_row, N)
                t = sec * SLOTS + i
                prod[t] = jnp.dot(adj_t[t], gbufs[h][slot], preferred_element_type=F32)

            yield

        @pl.loop(0, NT, unroll=2)
        def _(t):
            prod[t] = prod[t] + prod[chains[2, t]]

        yield

    def pair_terms(h):
        batch = links.batch(xterms[h])
        ends = [links.arrival() for _ in range(5)]
        for off in OFFSETS:
            zz = turn(z, off)
            for s in range(2):
                for sec in range(2):
                    value = prod[chains[3, sec * Q + zz * 2 + s]].astype(BF16)
                    for half in range(2):
                        terms[h][half, zz * 2 + s, pl.ds(sec * 64, 64)] = value[half * 64 : half * 64 + 64]
            chunk = pl.ds(zz * 2, 2)
            links.send(terms[h].at[1 - core, chunk], xterms[h].at[chunk], sibling, batch, ends[min(off, N - off)])
        return ends

    prod[NT] = jnp.zeros((TILE, TILE), F32)
    transpose(0)
    share0, share1 = share(0), share(1)
    step(share0)
    step(share1)
    transpose(1)
    chained.wait()
    step(share0, 2)
    step(share1, 2)
    step(share0)

    def sum_parts(h, slots, last):
        def fin(value):
            agg[h] = value.astype(BF16)

        return scatter_ring(links, parts[h], lambda p: None, slots, last, y, xl, y_ways, near_x, fin)

    forward0, forward1 = forward(0), forward(1)
    step(forward0)
    drain(share0)
    drain(forward0)
    sum0 = sum_parts(0, fslots0, flast0)
    step(sum0, 2)
    step(share1)
    step(forward1)
    drain(share1)
    drain(forward1)
    sum1 = sum_parts(1, fslots1, flast1)
    step(sum1)
    step(sum0)
    step(sum1, 2)
    drain(sum0)
    drain(sum1)

    pre = jnp.dot(agg[0], weight[pl.ds(0, TILE)], preferred_element_type=F32)
    pre = pre + jnp.dot(agg[1], weight[pl.ds(TILE, TILE)], preferred_element_type=F32)
    gate = jax.nn.sigmoid(pre)
    act_out[...] = (pre * gate).astype(BF16)
    gpre[...] = (gout[...].astype(F32) * gate * (1.0 + pre * (1.0 - gate))).astype(BF16)
    own = y * 2 + xl
    grads = []
    for h in range(2):
        gbufs[h][own] = lax.dot_general(
            gpre[...], weight[pl.ds(h * TILE, TILE)], (((1,), (1,)), ((), ())), preferred_element_type=F32
        ).astype(BF16)
        grads.append(gather_ring(links, gbufs[h], y, xl, y_ways, near_x))
        step(grads[h])

    gpre_t = gpre[...].T
    rows = 2 * TILE // Q
    for h in range(2):
        value = jnp.dot(gpre_t, agg[h], preferred_element_type=F32).astype(BF16)
        for p in range(Q):
            wt[(p % N) * 2 + p // N, :, pl.ds(h * TILE, TILE)] = value[p * rows : (p + 1) * rows]

    def weight_gradient():
        pair = []

        def fin(value):
            wsum[0] = value
            pair.append(links.send(wsum.at[0], wsum.at[1], sibling, links.batch(wsum.at[0])))

        yield from scatter_ring(links, wt, lambda p: None, wslots, wlast, y, xl, y_ways, near_x, fin)
        pair[0].wait_recv()
        wgather[place] = wsum[0] + wsum[1]
        yield from gather_ring(links, wgather, z, xh, z_ways, far_x)
        value = wgather[0]
        for q in range(1, Q):
            value = value + wgather[q]
        gw_out[...] = value
        yield

    wgrad = weight_gradient()
    step(wgrad, 2)
    step(grads[0], 2)
    step(grads[1], 2)
    step(wgrad)
    step(grads[0])
    backward0, backward1 = backward(0), backward(1)
    drain(backward0)

    def sum_terms(h, ends, slots, last):
        order = iter(OFFSETS)

        def prep(p):
            off = next(order)
            if off <= HALF:
                await_bytes(xterms[h].at[pl.ds(0, 2 if off in (0, HALF) else 4)], ends[off])
            for s in range(2):
                value = terms[h][core, p * 2 + s].astype(F32) + xterms[h][p * 2 + s].astype(F32)
                terms[h][core, p * 2 + s] = value.astype(BF16)

        def fin(value):
            for sec in range(2):
                gf_out[sec, :, pl.ds(h * TILE, TILE)] = value[sec * 64 : sec * 64 + 64]

        return scatter_ring(links, terms[h].at[core], prep, slots, last, z, xh, z_ways, far_x, fin)

    out0 = sum_terms(0, pair_terms(0), bslots0, blast0)
    step(wgrad)
    step(out0, 2)
    step(wgrad)
    drain(grads[1])
    drain(backward1)
    out1 = sum_terms(1, pair_terms(1), bslots1, blast1)
    step(out0)
    step(out1, 2)
    step(wgrad)
    step(out1)
    step(wgrad)
    drain(out0)
    drain(wgrad)
    drain(out1)
    links.finish()


def shards(features, adjacency, tile_ids, tile_counts, weight, grad_out):
    block = (TILE, TILE)
    hbm = pl.BlockSpec(memory_space=pltpu.HBM)
    vmem = pl.BlockSpec(memory_space=pltpu.VMEM)
    rows = 2 * TILE // Q
    stripe = (rows, 2 * TILE)
    slots, last = (2, 3), (9,)
    activated, grad_weight, grad_features = pl.pallas_call(
        kernel,
        out_shape=(
            pltpu.VMEM((TILE, 2 * TILE), BF16),
            pltpu.VMEM(stripe, F32),
            pltpu.VMEM((2, 64, 2 * TILE), F32),
        ),
        in_specs=[hbm] * 6,
        out_specs=(vmem, vmem, vmem),
        scratch_shapes=[
            pltpu.VMEM((2,) + block, BF16),
            pltpu.VMEM((1, 2, SLOTS) + block, BF16),
            pltpu.VMEM((2 * TILE, 2 * TILE), BF16),
            pltpu.VMEM((TILE, 2 * TILE), BF16),
            *[pltpu.VMEM((Q,) + block, BF16)] * 4,
            *[pltpu.VMEM((Q,) + block, BF16)] * 2,
            *[pltpu.VMEM((Q,) + block, BF16)] * 2,
            *[pltpu.VMEM((2, Q) + block, BF16)] * 2,
            *[pltpu.VMEM((Q,) + block, BF16)] * 2,
            pltpu.VMEM((NT,) + block, BF16),
            pltpu.VMEM((NT + 1,) + block, F32),
            pltpu.VMEM((2,) + block, BF16),
            pltpu.VMEM((TILE, 2 * TILE), BF16),
            *[pltpu.VMEM(slots + block, BF16)] * 2,
            *[pltpu.VMEM(last + block, BF16)] * 2,
            *[pltpu.VMEM(slots + block, BF16)] * 2,
            *[pltpu.VMEM(last + block, BF16)] * 2,
            pltpu.VMEM((Q,) + stripe, BF16),
            pltpu.VMEM(slots + stripe, BF16),
            pltpu.VMEM(last + stripe, BF16),
            pltpu.VMEM((2,) + stripe, F32),
            pltpu.VMEM((Q,) + stripe, F32),
            pltpu.SMEM((1, 2, SLOTS), jnp.int32),
            pltpu.SMEM((1, 2), jnp.int32),
            pltpu.VMEM((8, TILE), jnp.int32),
            pltpu.SMEM((8, TILE), jnp.int32),
            pltpu.SemaphoreType.DMA((8,)),
            pltpu.SemaphoreType.DMA((N_SEND,)),
            pltpu.SemaphoreType.DMA((N_RECV,)),
        ],
        compiler_params=pltpu.CompilerParams(
            collective_id=0, has_side_effects=True, vmem_limit_bytes=40 * 1024 * 1024
        ),
    )(*[pltpu.with_memory_space_constraint(x, pltpu.HBM) for x in (features, adjacency, tile_ids, tile_counts, weight, grad_out)])
    return activated, grad_weight.T, grad_features


def solution(mesh):
    return jax.shard_map(
        shards,
        mesh=mesh,
        in_specs=(
            P(("rows", "rep"), None),
            P("rows", "rep", None, None, None),
            P("rows", "rep", None),
            P("rows", "rep"),
            P(),
            P(("rows", "rep"), None),
        ),
        out_specs=(P(("rows", "rep"), None), P(None, "rep"), P("rep", "rows", None)),
        check_vma=False,
    )
```

time: 110 us -> 99.4 us (0.904)
  Pallas kernels: 105 us -> 96.5 us
  local copies, waits for them, and re-layouts: 3.49 us -> 1.89 us
    pallas_call x1, Pallas kernels: 105 us -> 96.5 us  [shards(): pl.pallas_call(kernel, out_shape=(pltpu.VMEM((TILE, 2 * TILE), BF16), plt...]
    unnamed x5 -> x3, local copies, waits for them, and re-layouts: 3.49 us -> 1.89 us
where the time goes in v3:
time: 99.4 us; the launch traced here: 99.1 us
  Pallas kernels  96.5 us (97%)
  local copies, waits for them, and re-layouts  1.89 us (2%)
    pallas_call x1, Pallas kernels, shards(): pl.pallas_call(kernel, out_shape=(pltpu.VMEM((TILE, 2 * TILE), BF16), plt...  96.5 us

profile of v3, /device:TPU:6, one launch (start us, length us, event | category | flops | bytes accessed | tf_op | source)
XLA Modules:
  0.0 99.1 jit_solution(13603161460168617341)
XLA Ops:
  0.6 96.5 %shard_map.85 = (bf16[128,256]{1,0:T(8,128)(2,1)S(1)}, f32[16,256]{1,0:T(8,128)S(1)}, f32[2,64,256]{2,1,0:T(8,128)S(1)}) custom-call(bf16[128,256]{1,0:T(8,128)(2,1)} %feat_in.1, bf16[1,2,16,128,128]{4,3,2,1,0:T(8,128)(2,1)} %adj_in.1, s32[1,2,16]{2,1,0:T(2,128)} %ids_in.1, s32[1,2]{1,0:T(1,128)} %counts_in.1, bf16[256,256]{1,0:T(8,128)(2,1)} %weight_in.1, ...), custom_call_target="tpu_custom_call" | custom-call | tf_op jit(solution)/shard_map/pallas_call | solution.py:447
  97.2 0.6 copy.12
  97.8 0.6 copy.13
  98.4 0.7 copy.14

commit v4 on v3

--- a/solution.py
+++ b/solution.py
@@ -11,12 +11,12 @@
 TILE = 128
 SLOTS = 16
 NT = 2 * SLOTS
-OFFSETS = (4, 3, 5, 1, 7, 0, 2, 6)
+OFFSETS = (4, 3, 5, 2, 6, 1, 7, 0)
 F32 = jnp.float32
 BF16 = jnp.bfloat16
 MESH = pl.DeviceIdType.MESH
-N_SEND = 16
-N_RECV = 80
+N_SEND = 17
+N_RECV = 112
 
 
 class Links:
@@ -61,48 +61,52 @@
 def gather_ring(links, buf, pos, sub, ways, partner, arrived=None):
     own = buf.at[pos * 2 + sub]
     batch = links.batch(buf.at[pl.ds(0, Q - 1)])
-    far = [[links.send(own, own, device, batch) for device in ways[1][side]] for side in range(2)]
-    close = [links.arrival() for _ in range(2)]
-    for side in range(2):
-        for device in ways[0][side]:
-            links.send(own, own, device, batch, close[side])
+    one = [[links.send(own, own, device, batch) for device in ways[0][side]] for side in range(2)]
     pair = links.send(own, own, partner, batch)
     yield
+
+    def blocks(side, distance):
+        p = lax.rem(pos + (N - distance, distance)[side], N)
+        return p, [buf.at[p * 2 + (sub if s == 0 else 1 - sub)] for s in range(2)]
+
+    two = []
+    for side in range(2):
+        p, came = blocks(side, 1)
+        moved = []
+        for s in range(2):
+            one[side][s].wait_recv()
+            moved.append(links.send(came[s], came[s], ways[0][side][0], batch))
+        two.append(moved)
+        if arrived:
+            arrived(p)
+    yield
     three, four = [links.arrival() for _ in range(2)], links.arrival()
     for side in range(2):
-        p = lax.rem(pos + (N - 2, 2)[side], N)
+        p, came = blocks(side, 2)
         for s in range(2):
-            far[side][s].wait_recv()
-            block = buf.at[p * 2 + (sub if s == 0 else 1 - sub)]
+            two[side][s].wait_recv()
             if s == side:
-                links.send(block, block, ways[1][side][0], batch, four)
-            links.send(block, block, ways[0][side][0], batch, three[side])
-    if arrived:
-        for side in range(2):
-            arrived(lax.rem(pos + (N - 2, 2)[side], N))
-    yield
-    two = buf.at[pl.ds(0, 2)]
+                links.send(came[s], came[s], ways[1][side][0], batch, four)
+            links.send(came[s], came[s], ways[0][side][0], batch, three[side])
+        if arrived:
+            arrived(p)
     pair.wait_recv()
     if arrived:
         arrived(pos)
-    for side in range(2):
-        await_bytes(two, close[side])
+    yield
+    for side in range(2):
+        await_bytes(buf.at[pl.ds(0, 2)], three[side])
         if arrived:
-            arrived(lax.rem(pos + (N - 1, 1)[side], N))
-    yield
-    for side in range(2):
-        await_bytes(two, three[side])
-        if arrived:
-            arrived(lax.rem(pos + (N - 3, 3)[side], N))
-    await_bytes(two, four)
+            arrived(blocks(side, 3)[0])
+    await_bytes(buf.at[pl.ds(0, 2)], four)
     if arrived:
         arrived(lax.rem(pos + HALF, N))
     yield
 
 
-def scatter_ring(links, own, prep, middle, last, pos, sub, ways, partner, done):
+def scatter_ring(links, own, prep, slots, last, pos, sub, ways, partner, done):
     batch, end = links.batch(own.at[pl.ds(0, Q - 1)]), links.arrival()
-    halfway = [links.arrival() for _ in range(2)]
+    at_two, at_one = [links.arrival() for _ in range(2)], [links.arrival() for _ in range(2)]
 
     def at(side, distance):
         return lax.rem(pos + (distance, N - distance)[side], N)
@@ -110,37 +114,38 @@
     p = at(0, HALF)
     prep(p)
     for side in range(2):
-        links.send(own.at[p * 2 + side], middle.at[side, 2], ways[1][side][0], batch, halfway[side])
+        links.send(own.at[p * 2 + side], slots.at[side, 2], ways[1][side][0], batch, at_two[side])
     for side in range(2):
         p = at(side, 3)
         prep(p)
-        links.send(own.at[pl.ds(p * 2, 2)], middle.at[side, pl.ds(0, 2)], ways[0][side][0], batch, halfway[side])
+        links.send(own.at[pl.ds(p * 2, 2)], slots.at[side, pl.ds(0, 2)], ways[0][side][0], batch, at_two[side])
+    yield
+    for side in range(2):
+        p = at(side, 2)
+        prep(p)
+        await_bytes(slots.at[side, pl.ds(0, 3)], at_two[side])
+        for s in range(2):
+            value = slots[side, s].astype(F32) + own[p * 2 + s].astype(F32)
+            if s == side:
+                value = value + slots[side, 2].astype(F32)
+            slots[side, s] = value.astype(BF16)
+        links.send(slots.at[side, pl.ds(0, 2)], slots.at[side, pl.ds(3, 2)], ways[0][side][0], batch, at_one[side])
     yield
     for side in range(2):
         p = at(side, 1)
         prep(p)
-        for t in range(2):
-            block = own.at[p * 2 + (sub if t == 0 else 1 - sub)]
-            links.send(block, last.at[side * 4 + t], ways[0][side][t], batch, end)
+        await_bytes(slots.at[side, pl.ds(3, 2)], at_one[side])
+        for s in range(2):
+            slots[side, 3 + s] = (slots[side, 3 + s].astype(F32) + own[p * 2 + s].astype(F32)).astype(BF16)
+        for t in (1, 0):
+            block = slots.at[side, 3 + (sub if t == 0 else 1 - sub)]
+            links.send(block, last.at[side * 2 + t], ways[0][side][t], batch, end)
     prep(pos)
-    links.send(own.at[pos * 2 + 1 - sub], last.at[8], partner, batch, end)
-    yield
-    for side in range(2):
-        p = at(side, 2)
-        prep(p)
-        await_bytes(middle.at[side], halfway[side])
-        for s in range(2):
-            value = middle[side, s].astype(F32) + own[p * 2 + s].astype(F32)
-            if s == side:
-                value = value + middle[side, 2].astype(F32)
-            middle[side, s] = value.astype(BF16)
-        for t in range(2):
-            block = middle.at[side, sub if t == 0 else 1 - sub]
-            links.send(block, last.at[side * 4 + 2 + t], ways[1][side][t], batch, end)
+    links.send(own.at[pos * 2 + 1 - sub], last.at[4], partner, batch, end)
     yield
     await_bytes(last, end)
     value = own[pos * 2 + sub].astype(F32)
-    for i in range(9):
+    for i in range(5):
         value = value + last[i].astype(F32)
     done(value)
     yield
@@ -164,7 +169,7 @@
     act_out, gw_out, gf_out,
     feat, adj, weight, gout, fown0, fown1, fpair0, fpair1, gbuf0, gbuf1, part0, part1, term0, term1, xterm0, xterm1, adj_t, prod, agg, gpre,
     fslots0, fslots1, flast0, flast1, bslots0, bslots1, blast0, blast1,
-    wt, wslots, wlast, wsum, wgather,
+    wt, wpair, wslots, wlast, wsum, wgather,
     ids, counts, table, chains, local_sems, send_sems, recv_sems,
 ):
     row, rep = lax.axis_index("rows"), lax.axis_index("rep")
@@ -322,14 +327,15 @@
         return ends
 
     prod[NT] = jnp.zeros((TILE, TILE), F32)
-    transpose(0)
     share0, share1 = share(0), share(1)
     step(share0)
+    transpose(0)
     step(share1)
     transpose(1)
     chained.wait()
-    step(share0, 2)
-    step(share1, 2)
+    for _ in range(2):
+        step(share0)
+        step(share1)
     step(share0)
 
     def sum_parts(h, slots, last):
@@ -343,15 +349,16 @@
     drain(share0)
     drain(forward0)
     sum0 = sum_parts(0, fslots0, flast0)
-    step(sum0, 2)
+    step(sum0)
     step(share1)
     step(forward1)
     drain(share1)
     drain(forward1)
     sum1 = sum_parts(1, fslots1, flast1)
+    for _ in range(2):
+        step(sum1)
+        step(sum0)
     step(sum1)
-    step(sum0)
-    step(sum1, 2)
     drain(sum0)
     drain(sum1)
 
@@ -374,29 +381,47 @@
     for h in range(2):
         value = jnp.dot(gpre_t, agg[h], preferred_element_type=F32).astype(BF16)
         for p in range(Q):
-            wt[(p % N) * 2 + p // N, :, pl.ds(h * TILE, TILE)] = value[p * rows : (p + 1) * rows]
+            wt[h, (p % N) * 2 + p // N] = value[p * rows : (p + 1) * rows]
 
     def weight_gradient():
-        pair = []
+        pair = links.send(wt.at[1 - core], wpair, sibling, links.batch(wpair))
+        yield
+        pair.wait_recv()
+        for q in range(Q):
+            wt[core, q] = (wt[core, q].astype(F32) + wpair[q].astype(F32)).astype(BF16)
 
         def fin(value):
-            wsum[0] = value
-            pair.append(links.send(wsum.at[0], wsum.at[1], sibling, links.batch(wsum.at[0])))
-
-        yield from scatter_ring(links, wt, lambda p: None, wslots, wlast, y, xl, y_ways, near_x, fin)
-        pair[0].wait_recv()
-        wgather[place] = wsum[0] + wsum[1]
-        yield from gather_ring(links, wgather, z, xh, z_ways, far_x)
-        value = wgather[0]
+            wgather[place] = value.astype(BF16)
+
+        ring = scatter_ring(links, wt.at[core], lambda p: None, wslots, wlast, y, xl, y_ways, near_x, fin)
+        for _ in range(3):
+            step(ring)
+            yield
+        drain(ring)
+        ring = gather_ring(links, wgather, z, xh, z_ways, far_x)
+        for _ in range(3):
+            step(ring)
+            yield
+        drain(ring)
+        value = wgather[0].astype(F32)
         for q in range(1, Q):
-            value = value + wgather[q]
-        gw_out[...] = value
+            value = value + wgather[q].astype(F32)
+        wsum[core] = value
+        half = wsum.at[core]
+        pair = links.send(half, half, sibling, links.batch(half))
         yield
+        pair.wait_recv()
+        for h in range(2):
+            gw_out[:, pl.ds(h * TILE, TILE)] = wsum[h]
+        yield
 
     wgrad = weight_gradient()
-    step(wgrad, 2)
-    step(grads[0], 2)
-    step(grads[1], 2)
+    step(wgrad)
+    step(grads[0])
+    step(wgrad)
+    step(grads[1])
+    step(grads[0])
+    step(grads[1])
     step(wgrad)
     step(grads[0])
     backward0, backward1 = backward(0), backward(1)
@@ -421,19 +446,22 @@
 
     out0 = sum_terms(0, pair_terms(0), bslots0, blast0)
     step(wgrad)
-    step(out0, 2)
-    step(wgrad)
+    step(out0)
     drain(grads[1])
     drain(backward1)
+    step(wgrad)
     out1 = sum_terms(1, pair_terms(1), bslots1, blast1)
     step(out0)
-    step(out1, 2)
-    step(wgrad)
     step(out1)
     step(wgrad)
+    step(out0)
+    step(out1)
+    step(wgrad)
     drain(out0)
+    step(out1)
+    step(wgrad)
+    drain(out1)
     drain(wgrad)
-    drain(out1)
     links.finish()
 
 
@@ -442,8 +470,8 @@
     hbm = pl.BlockSpec(memory_space=pltpu.HBM)
     vmem = pl.BlockSpec(memory_space=pltpu.VMEM)
     rows = 2 * TILE // Q
-    stripe = (rows, 2 * TILE)
-    slots, last = (2, 3), (9,)
+    stripe, part = (rows, 2 * TILE), (rows, TILE)
+    slots, last = (2, 5), (5,)
     activated, grad_weight, grad_features = pl.pallas_call(
         kernel,
         out_shape=(
@@ -471,11 +499,12 @@
             *[pltpu.VMEM(last + block, BF16)] * 2,
             *[pltpu.VMEM(slots + block, BF16)] * 2,
             *[pltpu.VMEM(last + block, BF16)] * 2,
-            pltpu.VMEM((Q,) + stripe, BF16),
-            pltpu.VMEM(slots + stripe, BF16),
-            pltpu.VMEM(last + stripe, BF16),
-            pltpu.VMEM((2,) + stripe, F32),
-            pltpu.VMEM((Q,) + stripe, F32),
+            pltpu.VMEM((2, Q) + part, BF16),
+            pltpu.VMEM((Q,) + part, BF16),
+            pltpu.VMEM(slots + part, BF16),
+            pltpu.VMEM(last + part, BF16),
+            pltpu.VMEM((2,) + part, F32),
+            pltpu.VMEM((Q,) + part, BF16),
             pltpu.SMEM((1, 2, SLOTS), jnp.int32),
             pltpu.SMEM((1, 2), jnp.int32),
             pltpu.VMEM((8, TILE), jnp.int32),

time: 99.4 us -> 95.7 us (0.963); the launches traced: 99.1 us -> 94.2 us
  Pallas kernels: 96.5 us -> 91.7 us
    pallas_call x1, Pallas kernels: 96.5 us -> 91.7 us  [shards(): pl.pallas_call(kernel, out_shape=(pltpu.VMEM((TILE, 2 * TILE), BF16), plt...]
where the time goes in v4:
time: 95.7 us; the launch traced here: 94.2 us
  Pallas kernels  91.7 us (96%)
  local copies, waits for them, and re-layouts  1.89 us (2%)
    pallas_call x1, Pallas kernels, shards(): pl.pallas_call(kernel, out_shape=(pltpu.VMEM((TILE, 2 * TILE), BF16), plt...  91.7 us

profile of v4, /device:TPU:6, one launch (start us, length us, event | category | flops | bytes accessed | tf_op | source)
XLA Modules:
  0.0 94.2 jit_solution(1546968722423081872)
XLA Ops:
  0.6 91.7 %shard_map.85 = (bf16[128,256]{1,0:T(8,128)(2,1)S(1)}, f32[16,256]{1,0:T(8,128)S(1)}, f32[2,64,256]{2,1,0:T(8,128)S(1)}) custom-call(bf16[128,256]{1,0:T(8,128)(2,1)} %feat_in.1, bf16[1,2,16,128,128]{4,3,2,1,0:T(8,128)(2,1)} %adj_in.1, s32[1,2,16]{2,1,0:T(2,128)} %ids_in.1, s32[1,2]{1,0:T(1,128)} %counts_in.1, bf16[256,256]{1,0:T(8,128)(2,1)} %weight_in.1, ...), custom_call_target="tpu_custom_call" | custom-call | tf_op jit(solution)/shard_map/pallas_call | solution.py:475
  92.3 0.6 copy.12
  92.9 0.6 copy.13
  93.5 0.7 copy.14

commit v5 on v4

--- a/solution.py
+++ b/solution.py
@@ -16,7 +16,7 @@
 BF16 = jnp.bfloat16
 MESH = pl.DeviceIdType.MESH
 N_SEND = 17
-N_RECV = 112
+N_RECV = 83
 
 
 class Links:
@@ -58,49 +58,59 @@
     pltpu.make_async_copy(ref, ref, sem).wait()
 
 
-def gather_ring(links, buf, pos, sub, ways, partner, arrived=None):
-    own = buf.at[pos * 2 + sub]
+def gather_ring(links, buf, pos, sub, ways, partner, straight=False, arrived=None):
+    own, two_blocks = buf.at[pos * 2 + sub], buf.at[pl.ds(0, 2)]
     batch = links.batch(buf.at[pl.ds(0, Q - 1)])
-    one = [[links.send(own, own, device, batch) for device in ways[0][side]] for side in range(2)]
-    pair = links.send(own, own, partner, batch)
-    yield
-
-    def blocks(side, distance):
-        p = lax.rem(pos + (N - distance, distance)[side], N)
-        return p, [buf.at[p * 2 + (sub if s == 0 else 1 - sub)] for s in range(2)]
-
-    two = []
+    came = [[links.arrival() for _ in range(2)] for _ in range(3)]
+    four, pair = links.arrival(), links.arrival()
+
+    def position(side, distance):
+        return lax.rem(pos + (N - distance, distance)[side], N)
+
+    for distance in (2, 1) if straight else (1,):
+        for t in (1, 0):
+            for side in range(2):
+                links.send(own, own, ways[distance - 1][side][t], batch, came[distance - 1][side])
+    links.send(own, own, partner, batch, pair)
+    yield
+
+    def first():
+        for side in range(2):
+            p = position(side, 1)
+            await_bytes(two_blocks, came[0][side])
+            if not straight:
+                chunk = buf.at[pl.ds(p * 2, 2)]
+                links.send(chunk, chunk, ways[0][side][0], batch, came[1][side])
+        if arrived:
+            for side in range(2):
+                arrived(position(side, 1))
+
+    if not straight:
+        first()
+        yield
     for side in range(2):
-        p, came = blocks(side, 1)
-        moved = []
-        for s in range(2):
-            one[side][s].wait_recv()
-            moved.append(links.send(came[s], came[s], ways[0][side][0], batch))
-        two.append(moved)
-        if arrived:
-            arrived(p)
-    yield
-    three, four = [links.arrival() for _ in range(2)], links.arrival()
-    for side in range(2):
-        p, came = blocks(side, 2)
-        for s in range(2):
-            two[side][s].wait_recv()
-            if s == side:
-                links.send(came[s], came[s], ways[1][side][0], batch, four)
-            links.send(came[s], came[s], ways[0][side][0], batch, three[side])
-        if arrived:
-            arrived(p)
-    pair.wait_recv()
+        p = position(side, 2)
+        await_bytes(two_blocks, came[1][side])
+        block, chunk = buf.at[p * 2 + (sub if side == 0 else 1 - sub)], buf.at[pl.ds(p * 2, 2)]
+        links.send(block, block, ways[1][side][0], batch, four)
+        links.send(chunk, chunk, ways[0][side][0], batch, came[2][side])
+    if arrived:
+        for side in range(2):
+            arrived(position(side, 2))
+    if straight:
+        yield
+        first()
+    await_bytes(own, pair)
     if arrived:
         arrived(pos)
     yield
     for side in range(2):
-        await_bytes(buf.at[pl.ds(0, 2)], three[side])
+        await_bytes(two_blocks, came[2][side])
         if arrived:
-            arrived(blocks(side, 3)[0])
-    await_bytes(buf.at[pl.ds(0, 2)], four)
+            arrived(position(side, 3))
+    await_bytes(two_blocks, four)
     if arrived:
-        arrived(lax.rem(pos + HALF, N))
+        arrived(position(0, HALF))
     yield
 
 
@@ -167,7 +177,7 @@
 def kernel(
     feat_in, adj_in, ids_in, counts_in, weight_in, gout_in,
     act_out, gw_out, gf_out,
-    feat, adj, weight, gout, fown0, fown1, fpair0, fpair1, gbuf0, gbuf1, part0, part1, term0, term1, xterm0, xterm1, adj_t, prod, agg, gpre,
+    feat, adj, weight, gout, fown0, fown1, fpair0, fpair1, gbuf0, gbuf1, part0, part1, term0, term1, xterm0, xterm1, adj_t, prod0, prod1, agg, gpre,
     fslots0, fslots1, flast0, flast1, bslots0, bslots1, blast0, blast1,
     wt, wpair, wslots, wlast, wsum, wgather,
     ids, counts, table, chains, local_sems, send_sems, recv_sems,
@@ -184,7 +194,7 @@
             + [(ids_in, ids), (counts_in, counts), (adj_in, adj), (weight_in, weight), (gout_in, gout)]
         )
     ]
-    for load in loads:
+    for load in loads[:2]:
         load.start()
 
     def device(z=z, xh=xh, core=core, xl=xl, y=y):
@@ -209,15 +219,18 @@
     source = device(z=sz, xh=sxh, xl=lax.rem(xh + xl + sxh, 2), y=turn(z, y - sz - HALF))
 
     barrier = pltpu.get_barrier_semaphore()
-    friends = [d for ways in (z_ways, y_ways) for sides in ways for side in sides for d in side]
+    friends = [d for ways in (z_ways, y_ways) for side in ways[0] for d in side]
+    friends += [*z_ways[1][0], *z_ways[1][1], y_ways[1][0][0], y_ways[1][1][0]]
     friends += [far_x, near_x, sibling, target, source]
     for friend in friends:
         pl.semaphore_signal(barrier, inc=1, device_id=friend, device_id_type=MESH)
+    for load in loads[2:]:
+        load.start()
     pl.semaphore_wait(barrier, len(friends))
 
     links = Links(send_sems, recv_sems)
     fowns, fpairs, gbufs, parts = (fown0, fown1), (fpair0, fpair1), (gbuf0, gbuf1), (part0, part1)
-    terms, xterms = (term0, term1), (xterm0, xterm1)
+    terms, xterms, prods = (term0, term1), (xterm0, xterm1), (prod0, prod1)
     batch = links.batch(feat)
     first = []
     for h in range(2):
@@ -228,12 +241,14 @@
 
     along = [lax.broadcasted_iota(jnp.int32, (NT, TILE), d) for d in range(2)]
 
+    sections = (core, 1 - core)
+
     def keys(t):
         name = jnp.zeros((NT, TILE), jnp.int32)
         for i in range(NT):
-            name = jnp.where(t == i, ids[0, i // SLOTS, i % SLOTS], name)
+            name = jnp.where(t == i, ids[0, sections[i // SLOTS], i % SLOTS], name)
         second = t >= SLOTS
-        live = t < jnp.where(second, counts[0, 1] + SLOTS, counts[0, 0])
+        live = t < jnp.where(second, counts[0, sections[1]] + SLOTS, counts[0, sections[0]])
         by_row = jnp.where(live, lax.shift_right_logical(name, 4), -1 - t)
         by_column = jnp.where(live, (name & (Q - 1)) + jnp.where(second, Q, 0), -1 - t)
         return by_row, by_column
@@ -252,10 +267,10 @@
     chained = pltpu.make_async_copy(table, chains, local_sems.at[7])
     chained.start()
 
-    def transpose(sec):
+    def transpose(part):
         @pl.loop(0, SLOTS, unroll=4)
         def _(i):
-            adj_t[sec * SLOTS + i] = adj[0, sec, i].T
+            adj_t[part * SLOTS + i] = adj[0, sections[part], i].T
 
     def share(h):
         end = links.arrival()
@@ -267,50 +282,38 @@
 
         def run():
             first[h].wait_recv()
-            yield from gather_ring(links, fowns[h], z, xh, z_ways, far_x, arrived)
+            yield from gather_ring(links, fowns[h], z, xh, z_ways, far_x, True, arrived)
             await_bytes(fpairs[h], end)
             yield
 
         return run()
 
     def forward(h):
-        for buf, sec in ((fowns[h], core), (fpairs[h], 1 - core)):
-
-            @pl.loop(0, SLOTS, unroll=4)
+        for part, buf in enumerate((fowns[h], fpairs[h])):
+            sec = sections[part]
+
+            @pl.loop(0, SLOTS, unroll=16)
             def _(i):
+                t = part * SLOTS + i
                 column = lax.rem(ids[0, sec, i], Q)
                 ez, exh = entry(sz, sxh, column // N, lax.rem(column, N))
-                prod[sec * SLOTS + i] = jnp.dot(adj[0, sec, i], buf[ez * 2 + exh], preferred_element_type=F32)
+                value = jnp.dot(adj[0, sec, i], buf[ez * 2 + exh], preferred_element_type=F32)
+                prods[h][t] = value + prods[h][chains[0, t]]
 
             yield
 
-        @pl.loop(0, NT, unroll=2)
-        def _(t):
-            prod[t] = prod[t] + prod[chains[0, t]]
-
-        for off in OFFSETS:
-            yy = turn(y, off)
-            for s in range(2):
-                parts[h][yy * 2 + s] = prod[chains[1, s * N + yy]].astype(BF16)
-        yield
-
     def backward(h):
-        for sec in range(2):
-
-            @pl.loop(0, SLOTS, unroll=4)
+        for part in range(2):
+
+            @pl.loop(0, SLOTS, unroll=16)
             def _(i):
-                tile_row = lax.div(ids[0, sec, i], Q)
+                t = part * SLOTS + i
+                tile_row = lax.div(ids[0, sections[part], i], Q)
                 slot = lax.rem(tile_row, N) * 2 + lax.div(tile_row, N)
-                t = sec * SLOTS + i
-                prod[t] = jnp.dot(adj_t[t], gbufs[h][slot], preferred_element_type=F32)
+                value = jnp.dot(adj_t[t], gbufs[h][slot], preferred_element_type=F32)
+                prods[h][t] = value + prods[h][chains[2, t]]
 
             yield
-
-        @pl.loop(0, NT, unroll=2)
-        def _(t):
-            prod[t] = prod[t] + prod[chains[2, t]]
-
-        yield
 
     def pair_terms(h):
         batch = links.batch(xterms[h])
@@ -319,14 +322,15 @@
             zz = turn(z, off)
             for s in range(2):
                 for sec in range(2):
-                    value = prod[chains[3, sec * Q + zz * 2 + s]].astype(BF16)
+                    value = prods[h][chains[3, lax.rem(sec + core, 2) * Q + zz * 2 + s]].astype(BF16)
                     for half in range(2):
                         terms[h][half, zz * 2 + s, pl.ds(sec * 64, 64)] = value[half * 64 : half * 64 + 64]
             chunk = pl.ds(zz * 2, 2)
             links.send(terms[h].at[1 - core, chunk], xterms[h].at[chunk], sibling, batch, ends[min(off, N - off)])
         return ends
 
-    prod[NT] = jnp.zeros((TILE, TILE), F32)
+    for prod in prods:
+        prod[NT] = jnp.zeros((TILE, TILE), F32)
     share0, share1 = share(0), share(1)
     step(share0)
     transpose(0)
@@ -342,7 +346,11 @@
         def fin(value):
             agg[h] = value.astype(BF16)
 
-        return scatter_ring(links, parts[h], lambda p: None, slots, last, y, xl, y_ways, near_x, fin)
+        def prep(p):
+            for s in range(2):
+                parts[h][p * 2 + s] = prods[h][chains[1, s * N + p]].astype(BF16)
+
+        return scatter_ring(links, parts[h], prep, slots, last, y, xl, y_ways, near_x, fin)
 
     forward0, forward1 = forward(0), forward(1)
     step(forward0)
@@ -360,9 +368,9 @@
         step(sum0)
     step(sum1)
     drain(sum0)
+
+    pre = jnp.dot(agg[0], weight[pl.ds(0, TILE)], preferred_element_type=F32)
     drain(sum1)
-
-    pre = jnp.dot(agg[0], weight[pl.ds(0, TILE)], preferred_element_type=F32)
     pre = pre + jnp.dot(agg[1], weight[pl.ds(TILE, TILE)], preferred_element_type=F32)
     gate = jax.nn.sigmoid(pre)
     act_out[...] = (pre * gate).astype(BF16)
@@ -463,6 +471,14 @@
     drain(out1)
     drain(wgrad)
     links.finish()
+
+
+def store(*refs):
+    copies = [pltpu.make_async_copy(refs[i], refs[3 + i], refs[6].at[i]) for i in range(3)]
+    for copy in copies:
+        copy.start()
+    for copy in copies:
+        copy.wait()
 
 
 def shards(features, adjacency, tile_ids, tile_counts, weight, grad_out):
@@ -492,7 +508,7 @@
             *[pltpu.VMEM((2, Q) + block, BF16)] * 2,
             *[pltpu.VMEM((Q,) + block, BF16)] * 2,
             pltpu.VMEM((NT,) + block, BF16),
-            pltpu.VMEM((NT + 1,) + block, F32),
+            *[pltpu.VMEM((NT + 1,) + block, F32)] * 2,
             pltpu.VMEM((2,) + block, BF16),
             pltpu.VMEM((TILE, 2 * TILE), BF16),
             *[pltpu.VMEM(slots + block, BF16)] * 2,
@@ -517,6 +533,14 @@
             collective_id=0, has_side_effects=True, vmem_limit_bytes=40 * 1024 * 1024
         ),
     )(*[pltpu.with_memory_space_constraint(x, pltpu.HBM) for x in (features, adjacency, tile_ids, tile_counts, weight, grad_out)])
+    results = (activated, grad_weight, grad_features)
+    activated, grad_weight, grad_features = pl.pallas_call(
+        store,
+        out_shape=[pltpu.HBM(x.shape, x.dtype) for x in results],
+        in_specs=[vmem] * 3,
+        out_specs=[hbm] * 3,
+        scratch_shapes=[pltpu.SemaphoreType.DMA((3,))],
+    )(*[pltpu.with_memory_space_constraint(x, pltpu.VMEM) for x in results])
     return activated, grad_weight.T, grad_features
 
 

time: 95.7 us -> 90.8 us (0.949)
  Pallas kernels: 91.7 us -> 89.5 us
  local copies, waits for them, and re-layouts: 1.89 us -> 0 us
    pallas_call x1, Pallas kernels: 91.7 us -> 88.8 us  [shards(): pl.pallas_call(kernel, out_shape=(pltpu.VMEM((TILE, 2 * TILE), BF16), plt...]
    unnamed x3 -> x0, local copies, waits for them, and re-layouts: 1.89 us -> none
where the time goes in v5:
time: 90.8 us; the launch traced here: 90.1 us
  Pallas kernels  89.5 us (99%)
    pallas_call x1, Pallas kernels, shards(): pl.pallas_call(kernel, out_shape=(pltpu.VMEM((TILE, 2 * TILE), BF16), plt...  88.8 us

profile of v5, /device:TPU:6, one launch (start us, length us, event | category | flops | bytes accessed | tf_op | source)
XLA Modules:
  0.0 90.1 jit_solution(2590987732641187386)
XLA Ops:
  0.6 88.8 %shard_map.85 = (bf16[128,256]{1,0:T(8,128)(2,1)S(1)}, f32[16,256]{1,0:T(8,128)S(1)}, f32[2,64,256]{2,1,0:T(8,128)S(1)}) custom-call(bf16[128,256]{1,0:T(8,128)(2,1)} %feat_in.1, bf16[1,2,16,128,128]{4,3,2,1,0:T(8,128)(2,1)} %adj_in.1, s32[1,2,16]{2,1,0:T(2,128)} %ids_in.1, s32[1,2]{1,0:T(1,128)} %counts_in.1, bf16[256,256]{1,0:T(8,128)(2,1)} %weight_in.1, ...), custom_call_target="tpu_custom_call" | custom-call | tf_op jit(solution)/shard_map/pallas_call | solution.py:491
  89.4 0.7 shard_map.86

commit v6 on v5

--- a/solution.py
+++ b/solution.py
@@ -219,9 +219,10 @@
     source = device(z=sz, xh=sxh, xl=lax.rem(xh + xl + sxh, 2), y=turn(z, y - sz - HALF))
 
     barrier = pltpu.get_barrier_semaphore()
-    friends = [d for ways in (z_ways, y_ways) for side in ways[0] for d in side]
+    friends = [source, target]
+    friends += [d for ways in (z_ways, y_ways) for side in ways[0] for d in side]
     friends += [*z_ways[1][0], *z_ways[1][1], y_ways[1][0][0], y_ways[1][1][0]]
-    friends += [far_x, near_x, sibling, target, source]
+    friends += [far_x, near_x, sibling]
     for friend in friends:
         pl.semaphore_signal(barrier, inc=1, device_id=friend, device_id_type=MESH)
     for load in loads[2:]:
@@ -268,7 +269,7 @@
     chained.start()
 
     def transpose(part):
-        @pl.loop(0, SLOTS, unroll=4)
+        @pl.loop(0, SLOTS, unroll=16)
         def _(i):
             adj_t[part * SLOTS + i] = adj[0, sections[part], i].T
 
@@ -453,11 +454,10 @@
         return scatter_ring(links, terms[h].at[core], prep, slots, last, z, xh, z_ways, far_x, fin)
 
     out0 = sum_terms(0, pair_terms(0), bslots0, blast0)
-    step(wgrad)
     step(out0)
     drain(grads[1])
     drain(backward1)
-    step(wgrad)
+    step(wgrad, 2)
     out1 = sum_terms(1, pair_terms(1), bslots1, blast1)
     step(out0)
     step(out1)

time: 90.8 us -> 90.3 us (level)
  no operation moved by 1% of the time
where the time goes in v6:
time: 90.3 us; the launch traced here: 89.9 us
  Pallas kernels  89.3 us (99%)
    pallas_call x1, Pallas kernels, shards(): pl.pallas_call(kernel, out_shape=(pltpu.VMEM((TILE, 2 * TILE), BF16), plt...  88.6 us

profile of v6, /device:TPU:6, one launch (start us, length us, event | category | flops | bytes accessed | tf_op | source)
XLA Modules:
  0.0 89.9 jit_solution(11260725251771868329)
XLA Ops:
  0.6 88.6 %shard_map.85 = (bf16[128,256]{1,0:T(8,128)(2,1)S(1)}, f32[16,256]{1,0:T(8,128)S(1)}, f32[2,64,256]{2,1,0:T(8,128)S(1)}) custom-call(bf16[128,256]{1,0:T(8,128)(2,1)} %feat_in.1, bf16[1,2,16,128,128]{4,3,2,1,0:T(8,128)(2,1)} %adj_in.1, s32[1,2,16]{2,1,0:T(2,128)} %ids_in.1, s32[1,2]{1,0:T(1,128)} %counts_in.1, bf16[256,256]{1,0:T(8,128)(2,1)} %weight_in.1, ...), custom_call_target="tpu_custom_call" | custom-call | tf_op jit(solution)/shard_map/pallas_call | solution.py:491
  89.2 0.7 shard_map.86

commit v7 on v6

--- a/solution.py
+++ b/solution.py
@@ -177,7 +177,7 @@
 def kernel(
     feat_in, adj_in, ids_in, counts_in, weight_in, gout_in,
     act_out, gw_out, gf_out,
-    feat, adj, weight, gout, fown0, fown1, fpair0, fpair1, gbuf0, gbuf1, part0, part1, term0, term1, xterm0, xterm1, adj_t, prod0, prod1, agg, gpre,
+    feat, adj, weight, weight_t, gout, fown0, fown1, fpair0, fpair1, gbuf0, gbuf1, part0, part1, term0, term1, xterm0, xterm1, adj_t, prod0, prod1, agg, gpre,
     fslots0, fslots1, flast0, flast1, bslots0, bslots1, blast0, blast1,
     wt, wpair, wslots, wlast, wsum, wgather,
     ids, counts, table, chains, local_sems, send_sems, recv_sems,
@@ -337,6 +337,7 @@
     transpose(0)
     step(share1)
     transpose(1)
+    weight_t[...] = weight[...].T
     chained.wait()
     for _ in range(2):
         step(share0)
@@ -374,17 +375,15 @@
     drain(sum1)
     pre = pre + jnp.dot(agg[1], weight[pl.ds(TILE, TILE)], preferred_element_type=F32)
     gate = jax.nn.sigmoid(pre)
-    act_out[...] = (pre * gate).astype(BF16)
     gpre[...] = (gout[...].astype(F32) * gate * (1.0 + pre * (1.0 - gate))).astype(BF16)
     own = y * 2 + xl
     grads = []
     for h in range(2):
-        gbufs[h][own] = lax.dot_general(
-            gpre[...], weight[pl.ds(h * TILE, TILE)], (((1,), (1,)), ((), ())), preferred_element_type=F32
-        ).astype(BF16)
+        gbufs[h][own] = jnp.dot(gpre[...], weight_t[:, pl.ds(h * TILE, TILE)], preferred_element_type=F32).astype(BF16)
         grads.append(gather_ring(links, gbufs[h], y, xl, y_ways, near_x))
         step(grads[h])
 
+    act_out[...] = (pre * gate).astype(BF16)
     gpre_t = gpre[...].T
     rows = 2 * TILE // Q
     for h in range(2):
@@ -500,7 +499,7 @@
         scratch_shapes=[
             pltpu.VMEM((2,) + block, BF16),
             pltpu.VMEM((1, 2, SLOTS) + block, BF16),
-            pltpu.VMEM((2 * TILE, 2 * TILE), BF16),
+            *[pltpu.VMEM((2 * TILE, 2 * TILE), BF16)] * 2,
             pltpu.VMEM((TILE, 2 * TILE), BF16),
             *[pltpu.VMEM((Q,) + block, BF16)] * 4,
             *[pltpu.VMEM((Q,) + block, BF16)] * 2,

time: 90.3 us -> 90.4 us (level)
  no operation moved by 1% of the time
where the time goes in v7:
time: 90.4 us; the launch traced here: 89.9 us
  Pallas kernels  89.3 us (99%)
    pallas_call x1, Pallas kernels, shards(): pl.pallas_call(kernel, out_shape=(pltpu.VMEM((TILE, 2 * TILE), BF16), plt...  88.5 us

profile of v7, /device:TPU:6, one launch (start us, length us, event | category | flops | bytes accessed | tf_op | source)
XLA Modules:
  0.0 89.9 jit_solution(1496483232964249118)
XLA Ops:
  0.6 88.5 %shard_map.85 = (bf16[128,256]{1,0:T(8,128)(2,1)S(1)}, f32[16,256]{1,0:T(8,128)S(1)}, f32[2,64,256]{2,1,0:T(8,128)S(1)}) custom-call(bf16[128,256]{1,0:T(8,128)(2,1)} %feat_in.1, bf16[1,2,16,128,128]{4,3,2,1,0:T(8,128)(2,1)} %adj_in.1, s32[1,2,16]{2,1,0:T(2,128)} %ids_in.1, s32[1,2]{1,0:T(1,128)} %counts_in.1, bf16[256,256]{1,0:T(8,128)(2,1)} %weight_in.1, ...), custom_call_target="tpu_custom_call" | custom-call | tf_op jit(solution)/shard_map/pallas_call | solution.py:490
  89.2 0.7 shard_map.86
